TPU v7x, 256 devices: a whole 4x4x8 slice. The times are simulated.
256 devices in a mesh: expert: 32 (over x, y, core), etp: 8 (over z).
Axes of the slice: x: 4, y: 4, z: 8, core: 2. Of those that a mesh axis runs over, the one named last changes fastest.
Arguments:
- tokens: bfloat16 [4096, 2048], P('expert', 'etp'), may hold values from -6 to 6
- grad_output: bfloat16 [4096, 2048], P('expert', 'etp'), may hold values from -2 to 2
- gates: bfloat16 [4096, 8], P('expert'), may hold values from 0.049804688 to 0.5
- ids: int32 [4096, 8], P('expert'), may hold values from 0 to 63, all different within a row; in each aligned block of 128 rows (0 to 127, 128 to 255, ...) at most 24 rows name the same one
- gate_weight: bfloat16 [64, 2048, 1024], P('expert', None, 'etp'), may hold values from -0.125 to 0.125
- up_weight: bfloat16 [64, 2048, 1024], P('expert', None, 'etp'), may hold values from -0.125 to 0.125
- down_weight: bfloat16 [64, 1024, 2048], P('expert', 'etp'), may hold values from -0.1875 to 0.1875
Outputs:
- grad_tokens: bfloat16 [4096, 2048], P('expert', 'etp')
- grad_gates: float32 [4096, 8], P('expert')
- grad_gate_weight: float32 [64, 2048, 1024], P('expert', None, 'etp')
- grad_up_weight: float32 [64, 2048, 1024], P('expert', None, 'etp')
- grad_down_weight: float32 [64, 1024, 2048], P('expert', 'etp')
Inputs may be any that keep to these rules, and one draw needn't show every extreme that they name: `ids`: in each aligned block of 128 tokens (those of one index of expert), no expert is named by more than 24 entries, a bound that some block reaches. The 8 experts of a token differ.
All inputs are finite; a program needn't handle non-finite values.
Results may differ from a plain program's by a relative error of at most 0.019.
Values may be sent and summed in bfloat16 or wider, within the bound.
A program may use at most 128 MiB of HBM per device.

v0:
```python
import jax
import jax.numpy as jnp
from jax import lax
from jax.sharding import PartitionSpec as P


def route_slots(id_block, expert_count, capacity):
    flat_ids = id_block.reshape(-1)
    onehot = (flat_ids[:, None] == jnp.arange(expert_count, dtype=jnp.int32)[None, :]).astype(
        jnp.int32
    )
    before = jnp.cumsum(onehot, axis=0) - onehot
    return flat_ids * capacity + jnp.sum(before * onehot, axis=1)


def local(tokens, grad_output, gates, ids, gate_weight, up_weight, down_weight):
    row_count, local_width = tokens.shape
    top_count = ids.shape[1]
    experts_here = gate_weight.shape[0]
    group_count = lax.axis_size("expert")
    expert_count = experts_here * group_count
    capacity = 3 * row_count * top_count // (2 * expert_count)
    slot_total = expert_count * capacity
    slots = route_slots(ids, expert_count, capacity)
    assigned = slots.shape[0]
    table = (
        jnp.full((slot_total,), assigned, jnp.int32)
        .at[slots]
        .set(jnp.arange(assigned, dtype=jnp.int32))
    )
    token_index = jnp.where(table < assigned, table // top_count, row_count)
    zero_row = jnp.zeros((1, local_width), jnp.bfloat16)
    token_send = jnp.concatenate([tokens, zero_row], axis=0)[token_index].reshape(
        expert_count, capacity, local_width
    )
    grad_send = jnp.concatenate([grad_output, zero_row], axis=0)[token_index].reshape(
        expert_count, capacity, local_width
    )
    gate_flat = jnp.concatenate([gates.reshape(-1), jnp.zeros((1,), jnp.bfloat16)])
    gate_send = gate_flat[table].reshape(expert_count, capacity)
    token_recv, grad_recv, gate_recv = (
        lax.all_to_all(token_send, "expert", split_axis=0, concat_axis=0, tiled=True),
        lax.all_to_all(grad_send, "expert", split_axis=0, concat_axis=0, tiled=True),
        lax.all_to_all(gate_send, "expert", split_axis=0, concat_axis=0, tiled=True),
    )
    token_full, grad_full = (
        lax.all_gather(token_recv, "etp", axis=2, tiled=True),
        lax.all_gather(grad_recv, "etp", axis=2, tiled=True),
    )
    model_width = token_full.shape[2]
    token_rows = token_full.reshape(group_count, experts_here, capacity, model_width)
    grad_rows = grad_full.reshape(group_count, experts_here, capacity, model_width)
    gate_col = gate_recv.reshape(group_count, experts_here, capacity, 1).astype(jnp.float32)
    gate_pre = jnp.einsum(
        "secd,edf->secf", token_rows, gate_weight, preferred_element_type=jnp.float32
    )
    up_pre = jnp.einsum("secd,edf->secf", token_rows, up_weight, preferred_element_type=jnp.float32)
    hidden_raw = jnp.einsum(
        "secd,efd->secf", grad_rows, down_weight, preferred_element_type=jnp.float32
    )
    sigmoid_gate = jax.nn.sigmoid(gate_pre)
    swish = gate_pre * sigmoid_gate
    hidden = swish * up_pre
    gate_part = jnp.sum(hidden * hidden_raw, axis=3)
    hidden_grad = gate_col * hidden_raw
    pre_up_grad = (hidden_grad * swish).astype(jnp.bfloat16)
    pre_gate_grad = (
        hidden_grad * up_pre * sigmoid_gate * (1.0 + gate_pre * (1.0 - sigmoid_gate))
    ).astype(jnp.bfloat16)
    scaled_hidden = (gate_col * hidden).astype(jnp.bfloat16)
    grad_down = jnp.einsum(
        "secf,secd->efd", scaled_hidden, grad_rows, preferred_element_type=jnp.float32
    )
    grad_gate = jnp.einsum(
        "secd,secf->edf", token_rows, pre_gate_grad, preferred_element_type=jnp.float32
    )
    grad_up = jnp.einsum(
        "secd,secf->edf", token_rows, pre_up_grad, preferred_element_type=jnp.float32
    )
    gate_total = lax.psum(gate_part, "etp")
    partial_value = (
        jnp.einsum("secf,edf->secd", pre_gate_grad, gate_weight, preferred_element_type=jnp.float32)
        + jnp.einsum("secf,edf->secd", pre_up_grad, up_weight, preferred_element_type=jnp.float32)
    ).astype(jnp.bfloat16)
    returned = lax.all_to_all(partial_value, "expert", split_axis=0, concat_axis=0, tiled=True)
    gate_back = lax.all_to_all(gate_total, "expert", split_axis=0, concat_axis=0, tiled=True)
    picked = returned.reshape(slot_total, model_width)[slots].astype(jnp.float32)
    token_sum = jnp.sum(picked.reshape(row_count, top_count, model_width), axis=1)
    grad_tokens = lax.psum_scatter(
        token_sum.astype(jnp.bfloat16), "etp", scatter_dimension=1, tiled=True
    )
    grad_gates = gate_back.reshape(slot_total)[slots].reshape(row_count, top_count)
    return (grad_tokens, grad_gates, grad_gate, grad_up, grad_down)


def solution(mesh):
    return jax.shard_map(
        local,
        mesh=mesh,
        in_specs=(
            P("expert", "etp"),
            P("expert", "etp"),
            P("expert", None),
            P("expert", None),
            P("expert", None, "etp"),
            P("expert", None, "etp"),
            P("expert", "etp", None),
        ),
        out_specs=(
            P("expert", "etp"),
            P("expert", None),
            P("expert", None, "etp"),
            P("expert", None, "etp"),
            P("expert", "etp", None),
        ),
        check_vma=False,
    )
```

profile of v0, /device:TPU:32, one launch (start us, length us, event | category | flops | bytes accessed | tf_op | source)
XLA Modules:
  0.0 408.7 jit_solution(9767067811218129740)
XLA Ops:
  7.2 0.0 copy-start
  7.2 0.0 copy-start.5
  7.2 0.0 all-gather.5.cloned.1.call-start
  7.2 0.8 broadcast_multiply_fusion
  8.0 0.8 copy.87
  8.8 0.1 eq.29
  8.9 0.1 eq.25
  9.0 0.1 copy.86
  9.1 0.1 mul.59
  9.2 18.0 %reduce-window.6 = s32[64,8,128]{2,1,0:T(8,128)S(1)} reduce-window(s32[64,8,128]{2,1,0:T(8,128)S(1)} %fusion.35, s32[]{:T(128)} %constant.13.clone.1), window={size=1x1x128 pad=0_0x0_0x127_0}, to_apply=%region_0.0 | reduce-window | flops 8323072 | bytes 524292 | tf_op jit(solution)/shard_map/reduce-window
  27.2 0.1 slice.18
  27.3 0.1 copy.89
  27.5 0.1 copy.90
  27.6 0.1 broadcast_add_fusion
  27.8 0.1 fusion.34
  27.9 4.3 %scatter_custom_fusion = s32[1536]{0:T(1024)S(1)} fusion(s32[1024]{0:T(1024)S(1)} %bitcast.73, s32[1024]{0:T(1024)S(1)} %iota.11, s32[]{:T(128)} %constant.16.clone.1), kind=kCustom, calls=%fused_computation.61 | custom fusion | bytes 6148 | tf_op jit(solution)/shard_map/scatter | solution.py:29
  32.2 0.8 concatenate.11
  33.1 4.8 %gather_fusion.2 = bf16[1536,256]{1,0:T(8,128)(2,1)S(1)} fusion(bf16[129,256]{1,0:T(8,128)(2,1)S(1)} %concatenate.11, s32[2048]{0:T(1024)S(1)} %get-tuple-element.35), kind=kCustom, calls=%fused_computation.2 | custom fusion | bytes 1579008 | tf_op jit(solution)/shard_map/gather | solution.py:33
  37.8 0.0 copy-start.7
  37.9 21.1 %all_to_all.29 = bf16[64,24,256]{2,1,0:T(8,128)(2,1)} all-to-all(bf16[64,24,256]{2,1,0:T(8,128)(2,1)S(1)} %bitcast.69), channel_id=1, replica_groups=mesh['expert'=32,'etp'=8] {'expert'}, dimensions={0} | all-to-all | bytes 1572864 | tf_op jit(solution)/shard_map/all_to_all | solution.py:42
  58.9 0.0 all-gather.5.cloned.1.call-update
  58.9 0.0 all-gather.3.cloned.1.call-start
  59.0 0.0 copy-done.5
  59.0 4.8 %gather_fusion.1 = bf16[1536,256]{1,0:T(8,128)(2,1)S(1)} fusion(bf16[129,256]{1,0:T(8,128)(2,1)S(1)} %concatenate.10, s32[2048]{0:T(1024)S(1)} %get-tuple-element.35), kind=kCustom, calls=%fused_computation.1 | custom fusion | bytes 1579008 | tf_op jit(solution)/shard_map/gather | solution.py:36
  63.8 18.0 %all_to_all.30 = bf16[64,24,256]{2,1,0:T(8,128)(2,1)} all-to-all(bf16[64,24,256]{2,1,0:T(8,128)(2,1)S(1)} %bitcast.68), channel_id=1, replica_groups=mesh['expert'=32,'etp'=8] {'expert'}, dimensions={0} | all-to-all | bytes 1572864 | tf_op jit(solution)/shard_map/all_to_all | solution.py:43
  81.8 0.0 all-gather.3.cloned.1.call-update
  81.8 0.0 copy-done.7
  81.8 0.1 copy.85
  81.9 0.1 reshape.93
  82.0 9.5 %gather_fusion = bf16[1536]{0:T(1024)(128)(2,1)S(1)} fusion(bf16[1025]{0:T(1024)(128)(2,1)S(1)} %pad_maximum_fusion, s32[2048]{0:T(1024)S(1)} %get-tuple-element.36), kind=kCustom, calls=%fused_computation | custom fusion | bytes 12288 | tf_op jit(solution)/shard_map/gather | solution.py:40
  91.5 0.0 copy-start.1
  91.5 0.1 all_to_all.18
  91.6 11.5 %all_to_all.31 = bf16[32,2,24]{2,1,0:T(2,128)(2,1)S(1)} all-to-all(bf16[32,2,24]{2,1,0:T(2,128)(2,1)S(1)} %all_to_all.18), channel_id=1, replica_groups=mesh['expert'=32,'etp'=8] {'expert'}, dimensions={0} | all-to-all | bytes 6144 | tf_op jit(solution)/shard_map/all_to_all | solution.py:44
  103.1 0.1 copy.91
  103.2 0.1 copy.92
  103.3 36.6 %all-gather.5.cloned.1.call-done = bf16[64,24,2048]{2,1,0:T(8,128)(2,1)} async-done(((bf16[64,24,256]{2,1,0:T(8,128)(2,1)}), bf16[64,24,2048]{2,1,0:T(8,128)(2,1)}) %all-gather.5.cloned.1.call-update) | async-done | bytes 6291472 | tf_op jit(solution)/shard_map/all_gather | solution.py:47
  139.9 0.0 copy-done
  139.9 5.7 %fusion.18 = f32[32,2,24,128]{3,2,0,1:T(8,128)} fusion(bf16[32,2,24,2048]{3,2,1,0:T(8,128)(2,1)} %bitcast.75, bf16[2,2048,128]{2,1,0:T(8,128)(2,1)S(1)} %copy-done), kind=kOutput, calls=%fused_computation.22 | convolution fusion | flops 805306368 | bytes 8126464 | tf_op jit(solution)/shard_map/secd,edf->secf/dot_general | solution.py:54
  145.6 0.0 copy-done.1
  145.6 2.8 fusion.15
  148.4 73.0 %all-gather.3.cloned.1.call-done = bf16[64,24,2048]{2,1,0:T(8,128)(2,1)} async-done(((bf16[64,24,256]{2,1,0:T(8,128)(2,1)}), bf16[64,24,2048]{2,1,0:T(8,128)(2,1)}) %all-gather.3.cloned.1.call-update) | async-done | bytes 6291472 | tf_op jit(solution)/shard_map/all_gather | solution.py:48
  221.3 6.6 %multiply_reduce_fusion = (f32[32,2,24]{2,0,1:T(8,128)}, bf16[32,2,24,128]{3,2,0,1:T(8,128)(2,1)S(1)}, bf16[32,2,24,128]{3,2,0,1:T(8,128)(2,1)}) fusion(f32[32,2,24,128]{3,2,0,1:T(8,128)} %fusion.15, f32[32,2,24,128]{3,2,0,1:T(8,128)} %fusion.18, f32[32,2,24]{2,0,1:T(8,128)S(1)} %copy.92, bf16[2,128,2048]{2,1,0:T(8,128)(2,1)S(1)} %copy-done.9, ...), kind=kOutput, calls=%fused_computation.30 | convolution fusion | flops 808647168 | bytes 9711616 | tf_op jit(solution)/shard_map/secd,efd->secf/dot_general | solution.py:58
  227.9 1.8 fusion.21
  229.8 0.0 copy-done.2
  229.8 2.9 fusion
  232.7 3.2 copy.96
  235.9 6.5 %all-to-all-start.3 = ((bf16[32,2,24,2048]{3,2,1,0:T(8,128)(2,1)}), bf16[32,2,24,2048]{3,2,1,0:T(8,128)(2,1)}, u32[]{:S(2)}, u32[]{:S(2)}) async-start(bf16[32,2,24,2048]{3,2,1,0:T(8,128)(2,1)} %copy.96), calls=%async_computation.3 | async-start | bytes 12582912 | tf_op jit(solution)/shard_map/all_to_all | solution.py:85
  242.4 0.3 reduce-scatter.2.cloned.1.call-start
  242.7 6.7 %convolution_bitcast_fusion.1 = f32[2,2048,128]{2,1,0:T(8,128)} fusion(bf16[32,2,24,2048]{3,2,1,0:T(8,128)(2,1)} %bitcast.76, bf16[32,2,24,128]{3,2,0,1:T(8,128)(2,1)S(1)} %copy-done.3), kind=kOutput, calls=%fused_computation.19 | convolution fusion | flops 805306368 | bytes 8781824 | tf_op jit(solution)/shard_map/secd,secf->edf/dot_general | solution.py:74
  249.4 72.9 %all-to-all-done.3 = bf16[32,2,24,2048]{3,2,1,0:T(8,128)(2,1)} async-done(((bf16[32,2,24,2048]{3,2,1,0:T(8,128)(2,1)}), bf16[32,2,24,2048]{3,2,1,0:T(8,128)(2,1)}, u32[]{:S(2)}, u32[]{:S(2)}) %all-to-all-start.3) | async-done | bytes 6291488 | tf_op jit(solution)/shard_map/all_to_all | solution.py:85
  322.3 12.5 %gather_fusion.3 = bf16[1024,2048]{1,0:T(8,128)(2,1)} fusion(bf16[1536,2048]{1,0:T(8,128)(2,1)} %bitcast.19, s32[1024]{0:T(1024)S(1)} %broadcast_clamp_fusion), kind=kCustom, calls=%fused_computation.3 | custom fusion | bytes 8392704 | tf_op jit(solution)/shard_map/gather | solution.py:87
  334.7 5.9 %bitcast_reduce_fusion = bf16[128,2048]{1,0:T(8,128)(2,1)} fusion(bf16[1024,2048]{1,0:T(8,128)(2,1)} %gather_fusion.3), kind=kLoop, calls=%fused_computation.16 | loop fusion | flops 1835008 | bytes 4718592 | tf_op jit(solution)/shard_map/reduce_sum | solution.py:88
  340.6 0.0 reduce-scatter.2.cloned.1.call-update
  340.6 0.0 copy-start.11
  340.7 6.8 %convolution_bitcast_fusion = f32[2,2048,128]{2,1,0:T(8,128)} fusion(bf16[32,2,24,2048]{3,2,1,0:T(8,128)(2,1)} %bitcast.77, bf16[32,2,24,128]{3,2,0,1:T(8,128)(2,1)S(1)} %copy-done.4), kind=kOutput, calls=%fused_computation.18 | convolution fusion | flops 805306368 | bytes 8781824 | tf_op jit(solution)/shard_map/secd,secf->edf/dot_general | solution.py:77
  347.4 26.9 %psum.7 = f32[32,2,24]{2,0,1:T(8,128)S(1)} all-reduce(f32[32,2,24]{2,0,1:T(8,128)S(1)} %copy-done.6), channel_id=1, replica_groups=mesh['expert'=32,'etp'=8] {'etp'}, use_global_device_ids=true, to_apply=%region_7.8 | all-reduce | flops 1536 | bytes 12288 | tf_op jit(solution)/shard_map/psum | solution.py:80
  374.4 0.6 copy.97
  375.0 12.7 %all-to-all-start.4 = ((f32[32,2,24]{2,1,0:T(2,128)}), f32[32,2,24]{2,1,0:T(2,128)S(1)}, u32[]{:S(2)}, u32[]{:S(2)}) async-start(f32[32,2,24]{2,1,0:T(2,128)} %copy.97), calls=%async_computation.5 | async-start | bytes 65536 | tf_op jit(solution)/shard_map/all_to_all | solution.py:86
  387.7 5.3 %fusion.9 = f32[2,128,2048]{2,1,0:T(8,128)} fusion(bf16[32,2,24,2048]{3,2,1,0:T(8,128)(2,1)} %bitcast.80, f32[32,2,24]{2,0,1:T(8,128)S(1)} %copy.92, f32[32,2,24,128]{3,2,0,1:T(8,128)S(1)} %copy-done.11, f32[32,2,24,128]{3,2,0,1:T(8,128)S(1)} %copy-done.10), kind=kOutput, calls=%fused_computation.17 | convolution fusion | flops 806682624 | bytes 9967616 | tf_op jit(solution)/shard_map/secf,secd->efd/dot_general | solution.py:71
  393.0 2.1 all-to-all-done.4
  395.1 0.1 reshape.100
  395.2 6.2 %gather_fusion.4 = f32[1024]{0:T(1024)S(1)} fusion(f32[1536]{0:T(1024)S(1)} %reshape.100, s32[1024]{0:T(1024)S(1)} %broadcast_clamp_fusion), kind=kCustom, calls=%fused_computation.4 | custom fusion | bytes 12288 | tf_op jit(solution)/shard_map/gather | solution.py:92
  401.4 0.1 reshape.101
  401.5 0.7 copy.101
  (25 shorter events, 0.1 us)
Async XLA Ops:
  7.2 132.7 %copy-start = (bf16[2,2048,128]{2,1,0:T(8,128)(2,1)S(1)}, bf16[2,2048,128]{2,1,0:T(8,128)(2,1)}, u32[]{:S(2)}) copy-start(bf16[2,2048,128]{2,1,0:T(8,128)(2,1)} %param.11) | copy-start | bytes 3145732
  7.2 51.8 %copy-start.5 = (bf16[128,256]{1,0:T(8,128)(2,1)S(1)}, bf16[128,256]{1,0:T(8,128)(2,1)}, u32[]{:S(2)}) copy-start(bf16[128,256]{1,0:T(8,128)(2,1)} %param.8) | copy-start | bytes 196612
  7.2 132.7 %all-gather.5.cloned.1.call-start = ((), (), s32[]{:S(2)}) async-start(), calls=%async_computation.7 | async-start | bytes 7077888 | tf_op jit(solution)/shard_map/all_gather | solution.py:47
  37.8 43.9 %copy-start.7 = (bf16[128,8]{0,1:T(8,128)(2,1)S(1)}, bf16[128,8]{0,1:T(8,128)(2,1)}, u32[]{:S(2)}) copy-start(bf16[128,8]{0,1:T(8,128)(2,1)} %param.9) | copy-start | bytes 6148
  58.9 162.4 %all-gather.3.cloned.1.call-start = ((), (), s32[]{:S(2)}) async-start(), calls=%async_computation.6 | async-start | bytes 7077888 | tf_op jit(solution)/shard_map/all_gather | solution.py:48
  91.5 54.1 %copy-start.1 = (bf16[2,2048,128]{2,1,0:T(8,128)(2,1)S(1)}, bf16[2,2048,128]{2,1,0:T(8,128)(2,1)}, u32[]{:S(2)}) copy-start(bf16[2,2048,128]{2,1,0:T(8,128)(2,1)} %param.12) | copy-start | bytes 3145732
  139.9 5.7 %copy-start.8 = (bf16[64,24,2048]{2,1,0:T(8,128)(2,1)S(1)}, bf16[64,24,2048]{2,1,0:T(8,128)(2,1)}, u32[]{:S(2)}) copy-start(bf16[64,24,2048]{2,1,0:T(8,128)(2,1)} %all-gather.5.cloned.1.call-done) | copy-start | bytes 18874372
  145.6 75.7 %copy-start.9 = (bf16[2,128,2048]{2,1,0:T(8,128)(2,1)S(1)}, bf16[2,128,2048]{2,1,0:T(8,128)(2,1)}, u32[]{:S(2)}) copy-start(bf16[2,128,2048]{2,1,0:T(8,128)(2,1)} %param.13) | copy-start | bytes 3145732
  227.9 1.9 copy-start.2
  235.9 6.8 %copy-start.3 = (bf16[32,2,24,128]{3,2,0,1:T(8,128)(2,1)S(1)}, bf16[32,2,24,128]{3,2,0,1:T(8,128)(2,1)}, u32[]{:S(2)}) copy-start(bf16[32,2,24,128]{3,2,0,1:T(8,128)(2,1)} %copy-done.2) | copy-start | bytes 1179652
  235.9 86.4 %all-to-all-start.3 = ((bf16[32,2,24,2048]{3,2,1,0:T(8,128)(2,1)}), bf16[32,2,24,2048]{3,2,1,0:T(8,128)(2,1)}, u32[]{:S(2)}, u32[]{:S(2)}) async-start(bf16[32,2,24,2048]{3,2,1,0:T(8,128)(2,1)} %copy.96), calls=%async_computation.3 | async-start | bytes 12582912 | tf_op jit(solution)/shard_map/all_to_all | solution.py:85
  242.4 159.7 %reduce-scatter.2.cloned.1.call-start = ((), (), s32[]{:S(2)}) async-start(), calls=%async_computation.8 | async-start | bytes 589824 | tf_op jit(solution)/shard_map/reduce_scatter | solution.py:89
  322.2 18.4 %copy-start.4 = (bf16[32,2,24,128]{3,2,0,1:T(8,128)(2,1)S(1)}, bf16[32,2,24,128]{3,2,0,1:T(8,128)(2,1)}, u32[]{:S(2)}) copy-start(bf16[32,2,24,128]{3,2,0,1:T(8,128)(2,1)} %get-tuple-element.32) | copy-start | bytes 1179652
  340.6 6.8 %copy-start.6 = (f32[32,2,24]{2,0,1:T(8,128)S(1)}, f32[32,2,24]{2,0,1:T(8,128)}, u32[]{:S(2)}) copy-start(f32[32,2,24]{2,0,1:T(8,128)} %get-tuple-element.30) | copy-start | bytes 18436
  340.6 47.1 %copy-start.10 = (f32[32,2,24,128]{3,2,0,1:T(8,128)S(1)}, f32[32,2,24,128]{3,2,0,1:T(8,128)}, u32[]{:S(2)}) copy-start(f32[32,2,24,128]{3,2,0,1:T(8,128)} %fusion.18) | copy-start | bytes 2359300
  340.6 47.1 %copy-start.11 = (f32[32,2,24,128]{3,2,0,1:T(8,128)S(1)}, f32[32,2,24,128]{3,2,0,1:T(8,128)}, u32[]{:S(2)}) copy-start(f32[32,2,24,128]{3,2,0,1:T(8,128)} %fusion.15) | copy-start | bytes 2359300
  375.0 20.1 %all-to-all-start.4 = ((f32[32,2,24]{2,1,0:T(2,128)}), f32[32,2,24]{2,1,0:T(2,128)S(1)}, u32[]{:S(2)}, u32[]{:S(2)}) async-start(f32[32,2,24]{2,1,0:T(2,128)} %copy.97), calls=%async_computation.5 | async-start | bytes 65536 | tf_op jit(solution)/shard_map/all_to_all | solution.py:86
Sparse Core Ops, SparseCore 0:
  59.1 80.7 all-gather.4
  141.6 79.6 all-gather.2
  340.7 41.3 reduce-scatter.1
where the time goes:
time: 413 us; the launch traced here: 409 us
  waiting for transfers between devices  185 us (45%)
  blocking collectives  77.5 us (19%)
  local copies, waits for them, and re-layouts  49.5 us (12%)
  matrix products  38.5 us (9%)
  other arithmetic  25 us (6%)
  starting transfers between devices  19.6 us (5%)
  between operations  14.1 us (3%)
    all_gather x1, waiting for transfers between devices, local(): lax.all_gather(grad_recv, 'etp', axis=2, tiled=True)  73 us
    all_to_all x1, waiting for transfers between devices, local(): lax.all_to_all(partial_value, 'expert', split_axis=0, concat_axis=0, tile...  72.9 us
    all_gather x1, waiting for transfers between devices, local(): lax.all_gather(token_recv, 'etp', axis=2, tiled=True)  36.6 us
    psum x1, blocking collectives, local(): gate_total = lax.psum(gate_part, 'etp')  26.9 us
    all_to_all x1, blocking collectives, local(): lax.all_to_all(token_send, 'expert', split_axis=0, concat_axis=0, tiled=T...  21.1 us
    another operation x3, other arithmetic  18.2 us
    all_to_all x1, blocking collectives, local(): lax.all_to_all(grad_send, 'expert', split_axis=0, concat_axis=0, tiled=True)  18 us
    all_to_all x1, starting transfers between devices, local(): lax.all_to_all(gate_total, 'expert', split_axis=0, concat_axis=0, tiled=T...  12.7 us
  transfers between devices with their start and end apart: 5, of which 4 were waited for; matrix products, arithmetic and copies ran while one was open for 12% of the time, Pallas kernels for 0%

commit v1 on v0

v1 whole, which is shorter than its diff:
```python
import functools

import jax
import jax.numpy as jnp
from jax import lax
from jax.experimental import pallas as pl
from jax.experimental.pallas import tpu as pltpu
from jax.sharding import PartitionSpec as P

MESH = pl.DeviceIdType.MESH
BF = jnp.bfloat16
F32 = jnp.float32
NX, NY, NZ = 4, 4, 8
TOK = 128
W = 256
D = 2048
H = 128
TOP = 8
CAP = 24
E4 = 4
PAIRS = 8
ROWS = 2 * CAP * PAIRS
SPLIT_T = (48, 32, 48)
SPLIT_G = (32, 48, 48)
SPLIT_R = (48, 32, 48)
COMPUTE = True


class Net:
    def __init__(self, send, recv):
        self.send_sem, self.recv_sem = send, recv
        self.count = 0
        self.pending = []

    def send(self, src, dst, device):
        k = self.count
        self.count += 1
        copy = pltpu.make_async_remote_copy(
            src_ref=src,
            dst_ref=dst,
            send_sem=self.send_sem.at[k],
            recv_sem=self.recv_sem.at[k],
            device_id=device,
            device_id_type=MESH,
        )
        copy.start()
        self.pending.append(copy)
        return copy

    def drain(self):
        for copy in self.pending:
            copy.wait_send()
        self.pending = []


def half16(n):
    return (n // 2 + 15) // 16 * 16


def ring4_gather(net, i, full, h0, h1, right, left):
    a = net.send(full(i), full(i), right)
    b = net.send(full(i), full(i), left)
    yield
    prev, following = lax.rem(i + 3, 4), lax.rem(i + 1, 4)
    a.wait_recv()
    c = net.send(h0(prev), h0(prev), right)
    b.wait_recv()
    d = net.send(h1(following), h1(following), left)
    yield
    c.wait_recv()
    d.wait_recv()
    yield


def ring8_gather(net, i, full, h0, h1, right, left):
    a = net.send(full(i), full(i), right)
    b = net.send(full(i), full(i), left)
    yield
    for step in (1, 2, 3):
        prev, following = lax.rem(i + 8 - step, 8), lax.rem(i + step, 8)
        va, vb = (full, full) if step < 3 else (h0, h1)
        a.wait_recv()
        a = net.send(va(prev), va(prev), right)
        b.wait_recv()
        b = net.send(vb(following), vb(following), left)
        yield
    a.wait_recv()
    b.wait_recv()
    yield


def add_into(dst, src):
    dst[...] = (dst[...].astype(F32) + src[...].astype(F32)).astype(BF)


def ring_scatter(net, n, i, full, h0, h1, slots, right, left):
    far = lax.rem(i + n // 2, n)
    ra, rb = slots[0]
    a = net.send(h0(far), ra, right)
    b = net.send(h1(far), rb, left)
    yield
    for step in range(1, n // 2):
        to_r, to_l = lax.rem(i + n // 2 - step, n), lax.rem(i + n // 2 + step, n)
        va, vb = (h0, h1) if step == 1 else (full, full)
        a.wait_recv()
        add_into(va(to_r), ra)
        ra, rb_next = slots[step]
        a = net.send(full(to_r), ra, right)
        b.wait_recv()
        add_into(vb(to_l), rb)
        rb = rb_next
        b = net.send(full(to_l), rb, left)
        yield
    a.wait_recv()
    b.wait_recv()
    dst = full(i)
    dst[...] = (dst[...].astype(F32) + ra[...].astype(F32) + rb[...].astype(F32)).astype(BF)
    yield


def run(*gens):
    for g in gens:
        next(g)


def scatter_slots():
    ra, rb, rc = SPLIT_R
    bc = rb + rc
    h = half16
    out = []

    def ring(n, half0, half1, whole):
        out.append([(half0, half1)] + [(whole, whole)] * (n // 2 - 1))

    ring(8, (2, 4, ra, W), (2, 4, ra, W), (4, 4, ra, W))
    ring(4, (2, ra, W), (2, ra, W), (4, ra, W))
    ring(4, (h(ra), W), (ra - h(ra), W), (ra, W))
    ring(4, (2, 8, rb, W), (2, 8, rb, W), (4, 8, rb, W))
    ring(4, (4, rb, W), (4, rb, W), (8, rb, W))
    ring(4, (2, 8, rc, W), (2, 8, rc, W), (4, 8, rc, W))
    ring(4, (4, rc, W), (4, rc, W), (8, rc, W))
    ring(8, (h(bc), W), (bc - h(bc), W), (bc, W))
    return out


N_SEM = 256
N_LOC = 32


def kernel(*refs):
    it = iter(refs)
    take = lambda n: [next(it) for _ in range(n)]
    tok_in, grad_in, rt_in, wg_in, wu_in, wd_in = take(6)
    tok_out, gg_out, dg_out, du_out, dd_out = take(5)
    gt, gg, xs, gxs, wgu, wd, sel, selt = take(8)
    pgu, sh, gp, member, target, gatev = take(6)
    rt, ggd, gg_rx, gg_rz = take(4)
    osg, osd, org, ord_ = take(4)
    stg, std = take(2)
    slots = [[tuple(take(2)) for _ in ring] for ring in scatter_slots()]
    send_sem, recv_sem, loc_sem, stg_sem = take(4)

    e_idx = lax.axis_index("expert")
    z = lax.axis_index("etp")
    core = lax.rem(e_idx, 2)
    y = lax.rem(e_idx // 2, 4)
    x = e_idx // 8

    def dev(dx=0, dy=0, xx=None, yy=None, cc=None, zz=None):
        px = lax.rem(x + dx + 4, 4) if xx is None else xx
        py = lax.rem(y + dy + 4, 4) if yy is None else yy
        pc = core if cc is None else cc
        return ((px * 4 + py) * 2 + pc, z if zz is None else zz)

    xr, xl = dev(dx=1), dev(dx=-1)
    yr, yl = dev(dy=1), dev(dy=-1)
    zr, zl = dev(zz=lax.rem(z + 1, 8)), dev(zz=lax.rem(z + 7, 8))
    x_far, y_far = dev(dx=2), dev(dy=2)
    x_near = dev(xx=x + 1 - 2 * lax.rem(x, 2))
    y_near = dev(yy=y + 1 - 2 * lax.rem(y, 2))
    z1 = dev(zz=z + 1 - 2 * lax.rem(z, 2))
    z2 = dev(zz=z + 2 - 4 * lax.rem(z // 2, 2))
    z4 = dev(zz=lax.rem(z + 4, 8))
    sibling = dev(cc=1 - core)

    own_copies = [
        pltpu.make_async_copy(tok_in, gt.at[x, y, z], loc_sem.at[0]),
        pltpu.make_async_copy(grad_in, gg.at[x, y, z], loc_sem.at[1]),
        pltpu.make_async_copy(rt_in, rt.at[x, y], loc_sem.at[2]),
    ]
    for j in range(2):
        ce = 2 * core + j
        own_copies.append(pltpu.make_async_copy(wg_in.at[j], wgu.at[ce, :, 0:H], loc_sem.at[3 + 3 * j]))
        own_copies.append(pltpu.make_async_copy(wu_in.at[j], wgu.at[ce, :, H : 2 * H], loc_sem.at[4 + 3 * j]))
        own_copies.append(pltpu.make_async_copy(wd_in.at[j], wd.at[ce], loc_sem.at[5 + 3 * j]))
    for c in own_copies:
        c.start()

    barrier = pltpu.get_barrier_semaphore()
    peers = (xr, xl, x_far, yr, yl, y_far, zr, zl, z2, z4, sibling)
    for p in peers:
        pl.semaphore_signal(barrier, inc=1, device_id=p, device_id_type=MESH)
    for c in own_copies[:3]:
        c.wait()
    pl.semaphore_wait(barrier, len(peers))

    net = Net(send_sem, recv_sem)

    class Wave:
        pass

    waves = []
    for buf, (ra, rb, rc) in ((gt, SPLIT_T), (gg, SPLIT_G)):
        w = Wave()
        a0, b0, c0 = 0, ra, ra + rb
        bc = rb + rc
        ha, hbc = half16(ra), half16(bc)
        w.xa = ring4_gather(
            net, x,
            lambda i, buf=buf, ra=ra: buf.at[i, y, z, pl.ds(0, ra)],
            lambda i, buf=buf, ha=ha: buf.at[i, y, z, pl.ds(0, ha)],
            lambda i, buf=buf, ha=ha, ra=ra: buf.at[i, y, z, pl.ds(ha, ra - ha)],
            xr, xl)
        w.ya = ring4_gather(
            net, y,
            lambda i, buf=buf, ra=ra: buf.at[:, i, z, pl.ds(0, ra)],
            lambda i, buf=buf, ra=ra: buf.at[pl.ds(0, 2), i, z, pl.ds(0, ra)],
            lambda i, buf=buf, ra=ra: buf.at[pl.ds(2, 2), i, z, pl.ds(0, ra)],
            yr, yl)
        w.za = ring8_gather(
            net, z,
            lambda i, buf=buf, ra=ra: buf.at[:, :, i, pl.ds(0, ra)],
            lambda i, buf=buf, ra=ra: buf.at[pl.ds(0, 2), :, i, pl.ds(0, ra)],
            lambda i, buf=buf, ra=ra: buf.at[pl.ds(2, 2), :, i, pl.ds(0, ra)],
            zr, zl)
        w.zbc = ring8_gather(
            net, z,
            lambda i, buf=buf, b0=b0, bc=bc: buf.at[x, y, i, pl.ds(b0, bc)],
            lambda i, buf=buf, b0=b0, h=hbc: buf.at[x, y, i, pl.ds(b0, h)],
            lambda i, buf=buf, b0=b0, h=hbc, bc=bc: buf.at[x, y, i, pl.ds(b0 + h, bc - h)],
            zr, zl)
        w.xb = ring4_gather(
            net, x,
            lambda i, buf=buf, b0=b0, rb=rb: buf.at[i, y, :, pl.ds(b0, rb)],
            lambda i, buf=buf, b0=b0, rb=rb: buf.at[i, y, pl.ds(0, 4), pl.ds(b0, rb)],
            lambda i, buf=buf, b0=b0, rb=rb: buf.at[i, y, pl.ds(4, 4), pl.ds(b0, rb)],
            xr, xl)
        w.yb = ring4_gather(
            net, y,
            lambda i, buf=buf, b0=b0, rb=rb: buf.at[:, i, :, pl.ds(b0, rb)],
            lambda i, buf=buf, b0=b0, rb=rb: buf.at[pl.ds(0, 2), i, :, pl.ds(b0, rb)],
            lambda i, buf=buf, b0=b0, rb=rb: buf.at[pl.ds(2, 2), i, :, pl.ds(b0, rb)],
            yr, yl)
        w.yc = ring4_gather(
            net, y,
            lambda i, buf=buf, c0=c0, rc=rc: buf.at[x, i, :, pl.ds(c0, rc)],
            lambda i, buf=buf, c0=c0, rc=rc: buf.at[x, i, pl.ds(0, 4), pl.ds(c0, rc)],
            lambda i, buf=buf, c0=c0, rc=rc: buf.at[x, i, pl.ds(4, 4), pl.ds(c0, rc)],
            yr, yl)
        w.xc = ring4_gather(
            net, x,
            lambda i, buf=buf, c0=c0, rc=rc: buf.at[i, :, :, pl.ds(c0, rc)],
            lambda i, buf=buf, c0=c0, rc=rc: buf.at[i, pl.ds(0, 2), :, pl.ds(c0, rc)],
            lambda i, buf=buf, c0=c0, rc=rc: buf.at[i, pl.ds(2, 2), :, pl.ds(c0, rc)],
            xr, xl)
        waves.append(w)
    wt, wgr = waves

    def both(name):
        run(*[getattr(w, name) for w in waves])

    both("xa")
    both("zbc")
    r = net.send(rt.at[x, y], rt.at[x, y], y_near)
    both("zbc")
    both("xa")
    r.wait_recv()
    yh = 2 * (y // 2)
    r = net.send(rt.at[x, pl.ds(yh, 2)], rt.at[x, pl.ds(yh, 2)], y_far)
    both("zbc")
    both("xa")
    both("ya")
    both("zbc")
    r.wait_recv()
    r = net.send(rt.at[x], rt.at[x], x_near)
    both("zbc")
    both("xb")
    both("yc")
    both("ya")
    both("ya")
    both("za")
    r.wait_recv()
    xh = 2 * (x // 2)
    r = net.send(rt.at[pl.ds(xh, 2)], rt.at[pl.ds(xh, 2)], x_far)
    for c in own_copies[3:]:
        c.wait()
    weight_copies = []
    for j in range(2):
        ce = 2 * core + j
        weight_copies.append(net.send(wgu.at[ce], wgu.at[ce], sibling))
        weight_copies.append(net.send(wd.at[ce], wd.at[ce], sibling))
    both("xb")
    both("yc")
    both("xb")
    both("yc")
    run(wt.yb, wt.xc)
    run(wgr.yb, wgr.xc)
    r.wait_recv()
    first_expert = 4 * (x * 4 + y)

    def route():
        for b in range(16):
            tile = rt[b // 4, b % 4]
            for e in range(E4):
                hit = tile[0:8, :] == (first_expert + e).astype(F32)
                member[e * 16 + b, :] = jnp.sum(jnp.where(hit, 1.0, 0.0), axis=0)
                gatev[e * 16 + b, :] = jnp.sum(jnp.where(hit, tile[8:16, :], 0.0), axis=0)
        tri = jnp.where(
            lax.broadcasted_iota(jnp.int32, (TOK, TOK), 0) < lax.broadcasted_iota(jnp.int32, (TOK, TOK), 1),
            1.0, 0.0).astype(BF)
        m = member[...]
        pos = jnp.dot(m.astype(BF), tri, preferred_element_type=F32)
        target[...] = jnp.where(m > 0.5, pos, -1.0)

        for p in range(PAIRS):
            row = lax.broadcasted_iota(jnp.int32, (CAP, TOK), 0).astype(F32)
            zero = jnp.zeros((CAP, TOK), F32)
            parts = []
            for e in range(E4):
                r0, r1 = e * 16 + 2 * p, e * 16 + 2 * p + 1
                s0 = jnp.where(row == target[r0 : r0 + 1, :], 1.0, 0.0)
                s1 = jnp.where(row == target[r1 : r1 + 1, :], 1.0, 0.0)
                parts.append(jnp.concatenate([s0, zero], axis=1))
                parts.append(jnp.concatenate([zero, s1], axis=1))
            full = jnp.concatenate(parts, axis=0)
            sel[p] = full.astype(BF)
            selt[p] = full.T.astype(BF)

    def pick(src, dst):
        def body(p, _):
            s = sel[p]
            px, py = p // 2, 2 * (p % 2)
            for zz in range(NZ):
                t = src[px, pl.ds(py, 2), zz].reshape(2 * TOK, W)
                o = jnp.dot(s, t, preferred_element_type=F32).astype(BF)
                for e in range(E4):
                    dst[e, pl.ds(pl.multiple_of(p * 48, 16), 48), zz * W : (zz + 1) * W] = o[e * 48 : (e + 1) * 48]
            return 0

        lax.fori_loop(0, PAIRS, body, 0)

    def forward(e):
        xe, ge = xs[e], gxs[e]
        gu = jnp.dot(xe, wgu[e], preferred_element_type=F32)
        raw = lax.dot_general(ge, wd[e], (((1,), (1,)), ((), ())), preferred_element_type=F32)
        gate_pre, up_pre = gu[:, :H], gu[:, H:]
        sig = 1.0 / (1.0 + jnp.exp(-gate_pre))
        swish = gate_pre * sig
        hidden = swish * up_pre
        gp[e] = jnp.broadcast_to(jnp.sum(hidden * raw, axis=1, keepdims=True), (ROWS, H))
        cols = []
        for p in range(PAIRS):
            for k in range(2):
                s = sel[p, pl.ds(pl.multiple_of(e * 48, 16), 48), k * TOK : (k + 1) * TOK].astype(F32)
                g = gatev[pl.ds(e * 16 + 2 * p + k, 1), :]
                cols.append(jnp.sum((s * g)[k * CAP : (k + 1) * CAP], axis=1, keepdims=True))
        gate = jnp.concatenate(cols, axis=0)
        hg = gate * raw
        pgu[e, :, H:] = (hg * swish).astype(BF)
        pgu[e, :, :H] = (hg * up_pre * sig * (1.0 + gate_pre * (1.0 - sig))).astype(BF)
        sh[e] = (gate * hidden).astype(BF)

    def partial(e):
        lhs = pgu[e]
        for zz in range(NZ):
            o = lax.dot_general(lhs, wgu[e, zz * W : (zz + 1) * W, :], (((1,), (1,)), ((), ())),
                                preferred_element_type=F32).astype(BF)
            for p in range(PAIRS):
                gg[p // 2, 2 * (p % 2) + e // 2, zz, pl.ds(pl.multiple_of((e % 2) * 48, 16), 48), :] = o[p * 48 : (p + 1) * 48]

    def spread(p):
        st = selt[p]
        px, py = p // 2, 2 * (p % 2)
        for zz in range(NZ):
            v = gg[px, pl.ds(py, 2), zz, 0:96, :].reshape(192, W)
            o = jnp.dot(st, v, preferred_element_type=F32).astype(BF)
            gt[px, pl.ds(py, 2), zz] = o.reshape(2, TOK, W)

    def gate_terms(p):
        for k in range(2):
            rows = []
            px, py = p // 2, 2 * (p % 2) + k
            tile = rt[px, py][0:8, :]
            acc = jnp.zeros((8, TOK), F32)
            for e in range(E4):
                s = sel[p, e * 48 : (e + 1) * 48, k * TOK : (k + 1) * TOK].astype(F32)
                v = jnp.sum(s * gp[e, pl.ds(pl.multiple_of(p * 48, 16), 48), :], axis=0, keepdims=True)
                acc = acc + jnp.where(tile == (first_expert + e).astype(F32), v, 0.0)
            ggd[px, py] = acc

    def loop(n, f):
        def body(i, _):
            f(i)
            return 0

        lax.fori_loop(0, n, body, 0)

    if COMPUTE:
        route()
    for _ in range(4):
        run(wt.za, wgr.za)
        if _ == 0:
            run(wt.yb, wt.xc, wgr.yb, wgr.xc)
    run(wt.yb, wt.xc, wgr.yb, wgr.xc)
    for c in weight_copies:
        c.wait_recv()
    net.drain()
    if COMPUTE:
        pick(gt, xs)
        pick(gg, gxs)
        loop(E4, forward)
        loop(E4, partial)
        loop(PAIRS, spread)
        loop(PAIRS, gate_terms)

    ra, rb, rc = SPLIT_R
    b0, c0, bc = ra, ra + rb, rb + rc
    ha, hbc = half16(ra), half16(bc)
    sz = pl.ds
    sza = ring_scatter(
        net, 8, z,
        lambda i: gt.at[:, :, i, sz(0, ra)],
        lambda i: gt.at[sz(0, 2), :, i, sz(0, ra)],
        lambda i: gt.at[sz(2, 2), :, i, sz(0, ra)],
        slots[0], zr, zl)
    sya = ring_scatter(
        net, 4, y,
        lambda i: gt.at[:, i, z, sz(0, ra)],
        lambda i: gt.at[sz(0, 2), i, z, sz(0, ra)],
        lambda i: gt.at[sz(2, 2), i, z, sz(0, ra)],
        slots[1], yr, yl)
    sxa = ring_scatter(
        net, 4, x,
        lambda i: gt.at[i, y, z, sz(0, ra)],
        lambda i: gt.at[i, y, z, sz(0, ha)],
        lambda i: gt.at[i, y, z, sz(ha, ra - ha)],
        slots[2], xr, xl)
    syb = ring_scatter(
        net, 4, y,
        lambda i: gt.at[:, i, :, sz(b0, rb)],
        lambda i: gt.at[sz(0, 2), i, :, sz(b0, rb)],
        lambda i: gt.at[sz(2, 2), i, :, sz(b0, rb)],
        slots[3], yr, yl)
    sxb = ring_scatter(
        net, 4, x,
        lambda i: gt.at[i, y, :, sz(b0, rb)],
        lambda i: gt.at[i, y, sz(0, 4), sz(b0, rb)],
        lambda i: gt.at[i, y, sz(4, 4), sz(b0, rb)],
        slots[4], xr, xl)
    sxc = ring_scatter(
        net, 4, x,
        lambda i: gt.at[i, :, :, sz(c0, rc)],
        lambda i: gt.at[i, sz(0, 2), :, sz(c0, rc)],
        lambda i: gt.at[i, sz(2, 2), :, sz(c0, rc)],
        slots[5], xr, xl)
    syc = ring_scatter(
        net, 4, y,
        lambda i: gt.at[x, i, :, sz(c0, rc)],
        lambda i: gt.at[x, i, sz(0, 4), sz(c0, rc)],
        lambda i: gt.at[x, i, sz(4, 4), sz(c0, rc)],
        slots[6], yr, yl)
    szbc = ring_scatter(
        net, 8, z,
        lambda i: gt.at[x, y, i, sz(b0, bc)],
        lambda i: gt.at[x, y, i, sz(b0, hbc)],
        lambda i: gt.at[x, y, i, sz(b0 + hbc, bc - hbc)],
        slots[7], zr, zl)

    def gate_ring():
        xo = 2 - 2 * (x // 2)
        c = net.send(ggd.at[sz(xo, 2)], gg_rx.at[sz(0, 2)], x_far)
        yield
        c.wait_recv()
        xm = 2 * (x // 2)
        for k in range(2):
            for j in range(4):
                ggd[xm + k, j] = ggd[xm + k, j] + gg_rx[k, j]
        xn = x + 1 - 2 * lax.rem(x, 2)
        c = net.send(ggd.at[xn], gg_rx.at[2], x_near)
        yield
        c.wait_recv()
        for j in range(4):
            ggd[x, j] = ggd[x, j] + gg_rx[2, j]
        yo = 2 - 2 * (y // 2)
        c = net.send(ggd.at[x, sz(yo, 2)], gg_rx.at[3, sz(0, 2)], y_far)
        yield
        c.wait_recv()
        ym = 2 * (y // 2)
        for k in range(2):
            ggd[x, ym + k] = ggd[x, ym + k] + gg_rx[3, k]
        yn = y + 1 - 2 * lax.rem(y, 2)
        c = net.send(ggd.at[x, yn], gg_rx.at[3, 2], y_near)
        yield
        c.wait_recv()
        gg_rz[0] = ggd[x, y] + gg_rx[3, 2]
        for k, d in enumerate((z1, z2, z4)):
            c = net.send(gg_rz.at[2 * k], gg_rz.at[2 * k + 1], d)
            yield
            c.wait_recv()
            gg_rz[2 * k + 2] = gg_rz[2 * k] + gg_rz[2 * k + 1]
        yield

    ring = gate_ring()
    run(sza, sxc, syb)
    run(ring)

    tn = (((0,), (0,)), ((), ()))

    def other_grads(j):
        e = 2 * (1 - core) + j

        def body(m, _):
            f = pl.ds(pl.multiple_of(m * W, W), W)
            osg[j, f, :] = lax.dot_general(xs[e, :, f], pgu[e], tn, preferred_element_type=F32).astype(BF)
            osd[j, :, f] = lax.dot_general(sh[e], gxs[e, :, f], tn, preferred_element_type=F32).astype(BF)
            return 0

        lax.fori_loop(0, NZ, body, 0)

    grad_copies = []
    if COMPUTE:
        for j in range(2):
            other_grads(j)
            grad_copies.append(net.send(osg.at[j], org.at[j], sibling))
            grad_copies.append(net.send(osd.at[j], ord_.at[j], sibling))
    run(sza, sxc, syb, ring)
    run(sza, ring)
    run(sxc, syb, ring)
    run(syc, sxb)
    run(sza, ring)
    run(syc, sxb, ring)
    run(sza, ring)
    run(syc, sxb, ring)
    run(sya, szbc)
    run(sya, szbc)
    run(sya, szbc)
    run(sxa, szbc)
    run(sxa, szbc)
    run(sxa)

    if COMPUTE:
        for c in grad_copies:
            c.wait_recv()

        def own_grads(t, _):
            j, m = t // NZ, t % NZ
            e = 2 * core + j
            f = pl.ds(pl.multiple_of(m * W, W), W)
            slot = lax.rem(t, 2)

            def outs(j, m, slot):
                f = pl.ds(pl.multiple_of(m * W, W), W)
                return [
                    pltpu.make_async_copy(stg.at[slot, :, 0:H], dg_out.at[j, f, :], stg_sem.at[slot, 0]),
                    pltpu.make_async_copy(stg.at[slot, :, H : 2 * H], du_out.at[j, f, :], stg_sem.at[slot, 1]),
                    pltpu.make_async_copy(std.at[slot], dd_out.at[j, :, f], stg_sem.at[slot, 2]),
                ]

            @pl.when(t >= 2)
            def _():
                for c in outs(j, m, slot):
                    c.wait()

            a = lax.dot_general(xs[e, :, f], pgu[e], tn, preferred_element_type=F32)
            stg[slot] = a + org[j, f, :].astype(F32)
            b = lax.dot_general(sh[e], gxs[e, :, f], tn, preferred_element_type=F32)
            std[slot] = b + ord_[j, :, f].astype(F32)
            for c in outs(j, m, slot):
                c.start()
            return 0

        lax.fori_loop(0, 2 * NZ, own_grads, 0)
        for slot in range(2):
            for c in (
                pltpu.make_async_copy(stg.at[slot, :, 0:H], dg_out.at[0, 0:W, :], stg_sem.at[slot, 0]),
                pltpu.make_async_copy(stg.at[slot, :, H : 2 * H], du_out.at[0, 0:W, :], stg_sem.at[slot, 1]),
                pltpu.make_async_copy(std.at[slot], dd_out.at[0, :, 0:W], stg_sem.at[slot, 2]),
            ):
                c.wait()

    tok_out[...] = gt[x, y, z]
    gg_out[...] = gg_rz[6]
    net.drain()


def local(tokens, grad_output, gates, ids, gate_weight, up_weight, down_weight):
    rt = jnp.concatenate([ids.astype(F32), gates.astype(F32)], axis=1).T
    any_spec = pl.BlockSpec(memory_space=pl.ANY)
    vmem = pl.BlockSpec(memory_space=pltpu.VMEM)
    big = (NX, NY, NZ, TOK, W)
    scratch = [
        pltpu.VMEM(big, BF),
        pltpu.VMEM(big, BF),
        pltpu.VMEM((E4, ROWS, D), BF),
        pltpu.VMEM((E4, ROWS, D), BF),
        pltpu.VMEM((E4, D, 2 * H), BF),
        pltpu.VMEM((E4, H, D), BF),
        pltpu.VMEM((PAIRS, 192, 2 * TOK), BF),
        pltpu.VMEM((PAIRS, 2 * TOK, 192), BF),
        pltpu.VMEM((E4, ROWS, 2 * H), BF),
        pltpu.VMEM((E4, ROWS, H), BF),
        pltpu.VMEM((E4, ROWS, H), F32),
        pltpu.VMEM((64, TOK), F32),
        pltpu.VMEM((64, TOK), F32),
        pltpu.VMEM((64, TOK), F32),
        pltpu.VMEM((NX, NY, 16, TOK), F32),
        pltpu.VMEM((NX, NY, 8, TOK), F32),
        pltpu.VMEM((4, 4, 8, TOK), F32),
        pltpu.VMEM((7, 8, TOK), F32),
        pltpu.VMEM((2, D, 2 * H), BF),
        pltpu.VMEM((2, H, D), BF),
        pltpu.VMEM((2, D, 2 * H), BF),
        pltpu.VMEM((2, H, D), BF),
        pltpu.VMEM((2, W, 2 * H), F32),
        pltpu.VMEM((2, H, W), F32),
    ]
    for ring in scatter_slots():
        for pair in ring:
            for shape in pair:
                scratch.append(pltpu.VMEM(shape, BF))
    scratch += [
        pltpu.SemaphoreType.DMA((N_SEM,)),
        pltpu.SemaphoreType.DMA((N_SEM,)),
        pltpu.SemaphoreType.DMA((N_LOC,)),
        pltpu.SemaphoreType.DMA((2, 3)),
    ]
    outs = pl.pallas_call(
        kernel,
        out_shape=(
            jax.ShapeDtypeStruct((TOK, W), BF),
            jax.ShapeDtypeStruct((8, TOK), F32),
            jax.ShapeDtypeStruct((2, D, H), F32),
            jax.ShapeDtypeStruct((2, D, H), F32),
            jax.ShapeDtypeStruct((2, H, D), F32),
        ),
        in_specs=[any_spec] * 6,
        out_specs=(vmem, vmem, any_spec, any_spec, any_spec),
        scratch_shapes=scratch,
        compiler_params=pltpu.CompilerParams(
            collective_id=0, has_side_effects=True, vmem_limit_bytes=63 * 1024 * 1024
        ),
    )(tokens, grad_output, rt, gate_weight, up_weight, down_weight)
    grad_tokens, gate_grads, grad_gate, grad_up, grad_down = outs
    return (grad_tokens, gate_grads.T, grad_gate, grad_up, grad_down)


def solution(mesh):
    return jax.shard_map(
        local,
        mesh=mesh,
        in_specs=(
            P("expert", "etp"),
            P("expert", "etp"),
            P("expert", None),
            P("expert", None),
            P("expert", None, "etp"),
            P("expert", None, "etp"),
            P("expert", "etp", None),
        ),
        out_specs=(
            P("expert", "etp"),
            P("expert", None),
            P("expert", None, "etp"),
            P("expert", None, "etp"),
            P("expert", "etp", None),
        ),
        check_vma=False,
    )
```

time: 413 us -> 196 us (0.47)
  waiting for transfers between devices: 185 us -> 0 us
  Pallas kernels: 0 us -> 183 us
  blocking collectives: 77.5 us -> 0 us
  local copies, waits for them, and re-layouts: 49.5 us -> 9.59 us
  matrix products: 38.5 us -> 0 us
  other arithmetic: 25 us -> 1.98 us
  starting transfers between devices: 19.6 us -> 0 us
  between operations: 14.1 us -> 0.64 us
    pallas_call x0 -> x1, Pallas kernels: none -> 183 us  [local(): pl.pallas_call(kernel, out_shape=(jax.ShapeDtypeStruct((TOK, W), BF), jax...]
    all_gather x2 -> x0, waiting for transfers between devices: 110 us -> none  [the longest x1 73 us: local(): lax.all_gather(grad_recv, 'etp', axis=2, tiled=True)]
    all_to_all x2 -> x0, waiting for transfers between devices: 75 us -> none  [the longest x1 72.9 us: local(): lax.all_to_all(partial_value, 'expert', split_axis=0, concat_axis=0, tile...]
    all_to_all x3 -> x0, blocking collectives: 50.5 us -> none  [the longest x1 21.1 us: local(): lax.all_to_all(token_send, 'expert', split_axis=0, concat_axis=0, tiled=T...]
    dot_general x8 -> x0, matrix products: 38.5 us -> none  [the longest x1 6.78 us: local(): jnp.einsum('secd,secf->edf', token_rows, pre_up_grad, preferred_element_t...]
    gather x5 -> x0, local copies, waits for them, and re-layouts: 37.6 us -> none  [the longest x1 12.5 us: local(): returned.reshape(slot_total, model_width)[slots].astype(jnp.float32)]
    psum x1 -> x0, blocking collectives: 26.9 us -> none  [local(): gate_total = lax.psum(gate_part, 'etp')]
    all_to_all x2 -> x0, starting transfers between devices: 19.2 us -> none  [the longest x1 12.7 us: local(): lax.all_to_all(gate_total, 'expert', split_axis=0, concat_axis=0, tiled=T...]
  transfers between devices with their start and end apart: 5 -> 0, of which waited for: 4 -> 0; matrix products, arithmetic and copies ran while one was open for 12% -> 0% of each run, Pallas kernels for 0% -> 0%
where the time goes in v1:
time: 196 us; the launch traced here: 195 us
  Pallas kernels  183 us (93%)
  local copies, waits for them, and re-layouts  9.59 us (5%)
  other arithmetic  1.98 us (1%)
    pallas_call x1, Pallas kernels, local(): pl.pallas_call(kernel, out_shape=(jax.ShapeDtypeStruct((TOK, W), BF), jax...  183 us
    unnamed x9, local copies, waits for them, and re-layouts  9.59 us

profile of v1, /device:TPU:32, one launch (start us, length us, event | category | flops | bytes accessed | tf_op | source)
XLA Modules:
  0.0 194.8 jit_solution(6052521580831825438)
XLA Ops:
  0.6 0.7 convert_element_type.7
  1.3 0.7 convert_element_type.6
  2.0 0.6 maximum_bitcast_fusion.refs_2_
  2.6 182.5 %shard_map.110 = (bf16[128,256]{1,0:T(8,128)(2,1)}, f32[8,128]{1,0:T(8,128)}, f32[2,2048,128]{2,1,0:T(8,128)}, f32[2,2048,128]{2,1,0:T(8,128)}, f32[2,128,2048]{2,1,0:T(8,128)}) custom-call(bf16[128,256]{1,0:T(8,128)(2,1)} %refs_0_.1, bf16[128,256]{1,0:T(8,128)(2,1)} %refs_1_.1, f32[16,128]{1,0:T(8,128)} %maximum_bitcast_fusion.refs_2_, ...), custom_call_target="tpu_custom_call" | custom-call | tf_op jit(solution)/shard_map/pallas_call | solution.py:637
  185.2 1.5 copy.17
  186.6 1.3 copy.18
  187.9 0.0 copy-start.1
  187.9 3.2 %copy.19 = f32[2,2048,128]{2,1,0:T(8,128)} copy(f32[2,2048,128]{2,1,0:T(8,128)} %get-tuple-element.22) | data formatting | bytes 4194304
  191.1 0.0 copy-done.1
  191.1 0.0 copy-start
  191.1 1.3 copy.20
  192.4 1.0 copy-done
  193.4 1.3 copy.21
Async XLA Ops:
  187.9 3.2 %copy-start.1 = (f32[2,2048,128]{2,1,0:T(8,128)S(1)}, f32[2,2048,128]{2,1,0:T(8,128)}, u32[]{:S(2)}) copy-start(f32[2,2048,128]{2,1,0:T(8,128)} %get-tuple-element.23) | copy-start | bytes 6291460
  191.1 2.3 %copy-start = (f32[2,128,2048]{2,1,0:T(8,128)S(1)}, f32[2,128,2048]{2,1,0:T(8,128)}, u32[]{:S(2)}) copy-start(f32[2,128,2048]{2,1,0:T(8,128)} %get-tuple-element.24) | copy-start | bytes 6291460

commit v2 on v1

v2 whole, which is shorter than its diff:
```python
import functools

import jax
import jax.numpy as jnp
from jax import lax
from jax.experimental import pallas as pl
from jax.experimental.pallas import tpu as pltpu
from jax.sharding import PartitionSpec as P

MESH = pl.DeviceIdType.MESH
BF = jnp.bfloat16
F32 = jnp.float32
NX, NY, NZ = 4, 4, 8
TOK = 128
W = 256
D = 2048
H = 128
TOP = 8
CAP = 24
E4 = 4
PAIRS = 8
ROWS = 2 * CAP * PAIRS
SPLIT_G = (48, 96, 112)
SPLIT_R = (32, 48, 48)
COMPUTE = True


class Net:
    def __init__(self, send, recv):
        self.send_sem, self.recv_sem = send, recv
        self.count = 0
        self.pending = []

    def send(self, src, dst, device):
        k = self.count
        self.count += 1
        copy = pltpu.make_async_remote_copy(
            src_ref=src,
            dst_ref=dst,
            send_sem=self.send_sem.at[k],
            recv_sem=self.recv_sem.at[k],
            device_id=device,
            device_id_type=MESH,
        )
        copy.start()
        self.pending.append(copy)
        return copy

    def drain(self):
        for copy in self.pending:
            copy.wait_send()
        self.pending = []


def half16(n):
    return (n // 2 + 15) // 16 * 16


def ring4_gather(net, i, full, h0, h1, right, left):
    a = net.send(full(i), full(i), right)
    b = net.send(full(i), full(i), left)
    yield
    prev, following = lax.rem(i + 3, 4), lax.rem(i + 1, 4)
    a.wait_recv()
    c = net.send(h0(prev), h0(prev), right)
    b.wait_recv()
    d = net.send(h1(following), h1(following), left)
    yield
    c.wait_recv()
    d.wait_recv()
    yield


def ring8_gather(net, i, full, h0, h1, right, left):
    a = net.send(full(i), full(i), right)
    b = net.send(full(i), full(i), left)
    yield
    for step in (1, 2, 3):
        prev, following = lax.rem(i + 8 - step, 8), lax.rem(i + step, 8)
        va, vb = (full, full) if step < 3 else (h0, h1)
        a.wait_recv()
        a = net.send(va(prev), va(prev), right)
        b.wait_recv()
        b = net.send(vb(following), vb(following), left)
        yield
    a.wait_recv()
    b.wait_recv()
    yield


def add_into(dst, src):
    dst[...] = (dst[...].astype(F32) + src[...].astype(F32)).astype(BF)


def ring_scatter(net, n, i, full, h0, h1, slots, right, left):
    far = lax.rem(i + n // 2, n)
    ra, rb = slots[0]
    a = net.send(h0(far), ra, right)
    b = net.send(h1(far), rb, left)
    yield
    for step in range(1, n // 2):
        to_r, to_l = lax.rem(i + n // 2 - step, n), lax.rem(i + n // 2 + step, n)
        va, vb = (h0, h1) if step == 1 else (full, full)
        a.wait_recv()
        add_into(va(to_r), ra)
        ra, rb_next = slots[step]
        a = net.send(full(to_r), ra, right)
        b.wait_recv()
        add_into(vb(to_l), rb)
        rb = rb_next
        b = net.send(full(to_l), rb, left)
        yield
    a.wait_recv()
    b.wait_recv()
    dst = full(i)
    dst[...] = (dst[...].astype(F32) + ra[...].astype(F32) + rb[...].astype(F32)).astype(BF)
    yield


def run(*gens):
    for g in gens:
        next(g)


def scatter_slots():
    ra, rb, rc = SPLIT_R
    h = half16
    out = []

    def ring(n, half0, half1, whole):
        out.append([(half0, half1)] + [(whole, whole)] * (n // 2 - 1))

    for _ in range(NZ):
        ring(4, (2, rc, W), (2, rc, W), (4, rc, W))
        ring(4, (2, rb, W), (2, rb, W), (4, rb, W))
    ring(8, (2, 4, ra, W), (2, 4, ra, W), (4, 4, ra, W))
    ring(8, (2, rb, W), (2, rb, W), (4, rb, W))
    ring(8, (2, rc, W), (2, rc, W), (4, rc, W))
    ring(4, (2, ra, W), (2, ra, W), (4, ra, W))
    ring(4, (h(ra), W), (ra - h(ra), W), (ra, W))
    ring(4, (h(rb), W), (rb - h(rb), W), (rb, W))
    ring(4, (h(rc), W), (rc - h(rc), W), (rc, W))
    return out


N_SEM = 320
N_LOC = 32


def kernel(*refs):
    it = iter(refs)
    take = lambda n: [next(it) for _ in range(n)]
    tok_in, grad_in, ids_in, gates_in, wg_in, wu_in, wd_in = take(7)
    tok_out, gg_out, dgu_out, dd_out = take(4)
    buf, xs, gxs, wgu, wd, sel, selt, part = take(8)
    agu, araw, pgu, sh, gp, member, target, gatev = take(8)
    rt, ggd, gg_rx, gg_rz = take(4)
    osg, osd, org, ord_ = take(4)
    stg, std = take(2)
    slots = [[tuple(take(2)) for _ in ring] for ring in scatter_slots()]
    send_sem, recv_sem, loc_sem, stg_sem = take(4)

    e_idx = lax.axis_index("expert")
    z = lax.axis_index("etp")
    core = lax.rem(e_idx, 2)
    y = lax.rem(e_idx // 2, 4)
    x = e_idx // 8

    def dev(dx=0, dy=0, xx=None, yy=None, cc=None, zz=None):
        px = lax.rem(x + dx + 4, 4) if xx is None else xx
        py = lax.rem(y + dy + 4, 4) if yy is None else yy
        pc = core if cc is None else cc
        return ((px * 4 + py) * 2 + pc, z if zz is None else zz)

    xr, xl = dev(dx=1), dev(dx=-1)
    yr, yl = dev(dy=1), dev(dy=-1)
    zr, zl = dev(zz=lax.rem(z + 1, 8)), dev(zz=lax.rem(z + 7, 8))
    x_far, y_far = dev(dx=2), dev(dy=2)
    x_near = dev(xx=x + 1 - 2 * lax.rem(x, 2))
    y_near = dev(yy=y + 1 - 2 * lax.rem(y, 2))
    z1 = dev(zz=z + 1 - 2 * lax.rem(z, 2))
    z2 = dev(zz=z + 2 - 4 * lax.rem(z // 2, 2))
    z4 = dev(zz=lax.rem(z + 4, 8))
    sibling = dev(cc=1 - core)

    own_copies = [
        pltpu.make_async_copy(tok_in, buf.at[x, y, z, pl.ds(0, TOK)], loc_sem.at[0]),
        pltpu.make_async_copy(grad_in, buf.at[x, y, z, pl.ds(TOK, TOK)], loc_sem.at[1]),
    ]
    for j in range(2):
        ce = 2 * core + j
        own_copies.append(pltpu.make_async_copy(wg_in.at[j], wgu.at[ce, :, 0:H], loc_sem.at[2 + 3 * j]))
        own_copies.append(pltpu.make_async_copy(wu_in.at[j], wgu.at[ce, :, H : 2 * H], loc_sem.at[3 + 3 * j]))
        own_copies.append(pltpu.make_async_copy(wd_in.at[j], wd.at[ce], loc_sem.at[4 + 3 * j]))
    for c in own_copies:
        c.start()

    rt[x, y, 0:8, :] = ids_in[...].astype(F32)
    rt[x, y, 8:16, :] = gates_in[...].astype(F32)
    barrier = pltpu.get_barrier_semaphore()
    peers = (xr, xl, x_far, yr, yl, y_far, zr, zl, z2, z4, sibling)
    for p in peers:
        pl.semaphore_signal(barrier, inc=1, device_id=p, device_id_type=MESH)
    for c in own_copies[:2]:
        c.wait()
    pl.semaphore_wait(barrier, len(peers))

    net = Net(send_sem, recv_sem)

    sz = pl.ds
    ra, rb, rc = SPLIT_G
    ga, gb, gab, gc = sz(0, ra), sz(ra, rb), sz(0, ra + rb), sz(ra + rb, rc)
    hab, hc = half16(ra + rb), half16(rc)
    zs = [z] + [lax.rem(z + k + 8, 8) for k in (1, -1, 2, -2, 3, -3, 4)]
    stage = [zs[0:1], zs[1:3], zs[3:5], zs[5:7], zs[7:8]]

    xab = ring4_gather(
        net, x,
        lambda i: buf.at[i, y, z, gab],
        lambda i: buf.at[i, y, z, sz(0, hab)],
        lambda i: buf.at[i, y, z, sz(hab, ra + rb - hab)],
        xr, xl)
    yc = ring4_gather(
        net, y,
        lambda i: buf.at[x, i, z, gc],
        lambda i: buf.at[x, i, z, sz(ra + rb, hc)],
        lambda i: buf.at[x, i, z, sz(ra + rb + hc, rc - hc)],
        yr, yl)
    ya = ring4_gather(
        net, y,
        lambda i: buf.at[:, i, z, ga],
        lambda i: buf.at[sz(0, 2), i, z, ga],
        lambda i: buf.at[sz(2, 2), i, z, ga],
        yr, yl)
    za = ring8_gather(
        net, z,
        lambda i: buf.at[:, :, i, ga],
        lambda i: buf.at[sz(0, 2), :, i, ga],
        lambda i: buf.at[sz(2, 2), :, i, ga],
        zr, zl)
    zb = ring8_gather(
        net, z,
        lambda i: buf.at[:, y, i, gb],
        lambda i: buf.at[sz(0, 2), y, i, gb],
        lambda i: buf.at[sz(2, 2), y, i, gb],
        zr, zl)
    zc = ring8_gather(
        net, z,
        lambda i: buf.at[x, :, i, gc],
        lambda i: buf.at[x, sz(0, 2), i, gc],
        lambda i: buf.at[x, sz(2, 2), i, gc],
        zr, zl)

    def plane(zz):
        return (
            ring4_gather(
                net, x,
                lambda i: buf.at[i, :, zz, gc],
                lambda i: buf.at[i, sz(0, 2), zz, gc],
                lambda i: buf.at[i, sz(2, 2), zz, gc],
                xr, xl),
            ring4_gather(
                net, y,
                lambda i: buf.at[:, i, zz, gb],
                lambda i: buf.at[sz(0, 2), i, zz, gb],
                lambda i: buf.at[sz(2, 2), i, zz, gb],
                yr, yl),
        )

    planes = [[plane(zz) for zz in group] for group in stage]

    def step(groups):
        for pair in groups:
            run(*pair)

    def route_ring():
        c = net.send(rt.at[x, y], rt.at[x, y], y_near)
        yield
        c.wait_recv()
        yh = 2 * (y // 2)
        c = net.send(rt.at[x, sz(yh, 2)], rt.at[x, sz(yh, 2)], y_far)
        yield
        c.wait_recv()
        c = net.send(rt.at[x], rt.at[x], x_near)
        yield
        c.wait_recv()
        xh = 2 * (x // 2)
        c = net.send(rt.at[sz(xh, 2)], rt.at[sz(xh, 2)], x_far)
        yield
        c.wait_recv()
        yield

    routing = route_ring()
    run(xab, yc, routing)
    run(xab, yc, routing)
    run(xab, yc)
    run(ya, zb, zc)
    step(planes[0])
    run(routing, ya)
    for c in own_copies[2:]:
        c.wait()
    weight_copies = []
    for j in range(2):
        ce = 2 * core + j
        weight_copies.append(net.send(wgu.at[ce], wgu.at[ce], sibling))
        weight_copies.append(net.send(wd.at[ce], wd.at[ce], sibling))
    run(ya)
    run(routing)
    step(planes[0])
    run(routing)
    first_expert = 4 * (x * 4 + y)

    def route():
        for b in range(16):
            tile = rt[b // 4, b % 4]
            for e in range(E4):
                hit = tile[0:8, :] == (first_expert + e).astype(F32)
                member[e * 16 + b, :] = jnp.sum(jnp.where(hit, 1.0, 0.0), axis=0)
                gatev[e * 16 + b, :] = jnp.sum(jnp.where(hit, tile[8:16, :], 0.0), axis=0)
        tri = jnp.where(
            lax.broadcasted_iota(jnp.int32, (TOK, TOK), 0) < lax.broadcasted_iota(jnp.int32, (TOK, TOK), 1),
            1.0, 0.0).astype(BF)
        m = member[...]
        pos = jnp.dot(m.astype(BF), tri, preferred_element_type=F32)
        target[...] = jnp.where(m > 0.5, pos, -1.0)

        for p in range(PAIRS):
            row = lax.broadcasted_iota(jnp.int32, (CAP, TOK), 0).astype(F32)
            zero = jnp.zeros((CAP, TOK), F32)
            parts = []
            for e in range(E4):
                r0, r1 = e * 16 + 2 * p, e * 16 + 2 * p + 1
                s0 = jnp.where(row == target[r0 : r0 + 1, :], 1.0, 0.0)
                s1 = jnp.where(row == target[r1 : r1 + 1, :], 1.0, 0.0)
                parts.append(jnp.concatenate([s0, zero], axis=1))
                parts.append(jnp.concatenate([zero, s1], axis=1))
            full = jnp.concatenate(parts, axis=0)
            sel[p] = full.astype(BF)
            selt[p] = full.T.astype(BF)

    def pick(zz):
        def body(px, _):
            for q in range(2):
                p = 2 * px + q
                s = sel[p]
                for r0, dst in ((0, xs), (TOK, gxs)):
                    t = buf[px, 2 * q : 2 * q + 2, zz, r0 : r0 + TOK, :].reshape(2 * TOK, W)
                    o = jnp.dot(s, t, preferred_element_type=F32).astype(BF)
                    for e in range(E4):
                        dst[zz, e, pl.ds(pl.multiple_of(p * 48, 16), 48), :] = o[e * 48 : (e + 1) * 48]
            return 0

        lax.fori_loop(0, PAIRS // 2, body, 0)

    def accumulate(zz, first):
        f = pl.ds(pl.multiple_of(zz * W, W), W)

        def body(e):
            gu = jnp.dot(xs[zz, e], wgu[e, f, :], preferred_element_type=F32)
            raw = lax.dot_general(gxs[zz, e], wd[e, :, f], (((1,), (1,)), ((), ())), preferred_element_type=F32)
            if first:
                agu[e] = gu
                araw[e] = raw
            else:
                agu[e] += gu
                araw[e] += raw

        for e in range(E4):
            body(e)

    def consume(group, first=False):
        if COMPUTE:
            for zz in group:
                pick(zz)
                accumulate(zz, first)

    def forward(e):
        gu, raw = agu[e], araw[e]
        gate_pre, up_pre = gu[:, :H], gu[:, H:]
        sig = 1.0 / (1.0 + jnp.exp(-gate_pre))
        swish = gate_pre * sig
        hidden = swish * up_pre
        gp[e] = jnp.broadcast_to(jnp.sum(hidden * raw, axis=1, keepdims=True), (ROWS, H))
        cols = []
        for p in range(PAIRS):
            for k in range(2):
                s = sel[p, pl.ds(pl.multiple_of(e * 48, 16), 48), k * TOK : (k + 1) * TOK].astype(F32)
                g = gatev[pl.ds(e * 16 + 2 * p + k, 1), :]
                cols.append(jnp.sum((s * g)[k * CAP : (k + 1) * CAP], axis=1, keepdims=True))
        gate = jnp.concatenate(cols, axis=0)
        hg = gate * raw
        pgu[e, :, H:] = (hg * swish).astype(BF)
        pgu[e, :, :H] = (hg * up_pre * sig * (1.0 + gate_pre * (1.0 - sig))).astype(BF)
        sh[e] = (gate * hidden).astype(BF)

    def produce(zz):
        f = pl.ds(pl.multiple_of(zz * W, W), W)

        def products(e):
            o = lax.dot_general(pgu[e], wgu[e, f, :], (((1,), (1,)), ((), ())),
                                preferred_element_type=F32).astype(BF)
            for p in range(PAIRS):
                part[p, e * 48 : (e + 1) * 48, :] = o[p * 48 : (p + 1) * 48]

        def spread(p, _):
            for q in range(4):
                o = jnp.dot(selt[4 * p + q], part[4 * p + q], preferred_element_type=F32).astype(BF)
                buf[2 * p + q // 2, 2 * (q % 2) : 2 * (q % 2) + 2, zz, 0:TOK, :] = o.reshape(2, TOK, W)
            return 0

        if COMPUTE:
            for e in range(E4):
                products(e)
            lax.fori_loop(0, PAIRS // 4, spread, 0)

    def gate_terms(p):
        for k in range(2):
            rows = []
            px, py = p // 2, 2 * (p % 2) + k
            tile = rt[px, py][0:8, :]
            acc = jnp.zeros((8, TOK), F32)
            for e in range(E4):
                s = sel[p, e * 48 : (e + 1) * 48, k * TOK : (k + 1) * TOK].astype(F32)
                v = jnp.sum(s * gp[e, pl.ds(pl.multiple_of(p * 48, 16), 48), :], axis=0, keepdims=True)
                acc = acc + jnp.where(tile == (first_expert + e).astype(F32), v, 0.0)
            ggd[px, py] = acc

    def loop(n, f):
        def body(i, _):
            f(i)
            return 0

        lax.fori_loop(0, n, body, 0)

    if COMPUTE:
        route()
    for c in weight_copies:
        c.wait_recv()
    for k in range(1, 5):
        run(zb, zc)
        step(planes[k])
        step(planes[k - 1])
        run(za)
        consume(stage[k - 1], k == 1)
        step(planes[k])
    step(planes[4])
    run(za)
    consume(stage[4])
    net.drain()
    if COMPUTE:
        loop(E4, forward)

    ra, rb, rc = SPLIT_R
    sa, sb, sc = sz(0, ra), sz(ra, rb), sz(ra + rb, rc)
    ha, hb, hc = half16(ra), half16(rb), half16(rc)

    def rplane(k, zz):
        return (
            ring_scatter(
                net, 4, x,
                lambda i: buf.at[i, :, zz, sc],
                lambda i: buf.at[i, sz(0, 2), zz, sc],
                lambda i: buf.at[i, sz(2, 2), zz, sc],
                slots[2 * k], xr, xl),
            ring_scatter(
                net, 4, y,
                lambda i: buf.at[:, i, zz, sb],
                lambda i: buf.at[sz(0, 2), i, zz, sb],
                lambda i: buf.at[sz(2, 2), i, zz, sb],
                slots[2 * k + 1], yr, yl),
        )

    back = [rplane(k, zz) for k, zz in enumerate(zs)]
    back = [back[0:1], back[1:3], back[3:5], back[5:7], back[7:8]]
    slots = slots[16:]
    sza = ring_scatter(
        net, 8, z,
        lambda i: buf.at[:, :, i, sa],
        lambda i: buf.at[sz(0, 2), :, i, sa],
        lambda i: buf.at[sz(2, 2), :, i, sa],
        slots[0], zr, zl)
    szb = ring_scatter(
        net, 8, z,
        lambda i: buf.at[:, y, i, sb],
        lambda i: buf.at[sz(0, 2), y, i, sb],
        lambda i: buf.at[sz(2, 2), y, i, sb],
        slots[1], zr, zl)
    szc = ring_scatter(
        net, 8, z,
        lambda i: buf.at[x, :, i, sc],
        lambda i: buf.at[x, sz(0, 2), i, sc],
        lambda i: buf.at[x, sz(2, 2), i, sc],
        slots[2], zr, zl)
    sya = ring_scatter(
        net, 4, y,
        lambda i: buf.at[:, i, z, sa],
        lambda i: buf.at[sz(0, 2), i, z, sa],
        lambda i: buf.at[sz(2, 2), i, z, sa],
        slots[3], yr, yl)
    sxa = ring_scatter(
        net, 4, x,
        lambda i: buf.at[i, y, z, sa],
        lambda i: buf.at[i, y, z, sz(0, ha)],
        lambda i: buf.at[i, y, z, sz(ha, ra - ha)],
        slots[4], xr, xl)
    sxb = ring_scatter(
        net, 4, x,
        lambda i: buf.at[i, y, z, sb],
        lambda i: buf.at[i, y, z, sz(ra, hb)],
        lambda i: buf.at[i, y, z, sz(ra + hb, rb - hb)],
        slots[5], xr, xl)
    syc = ring_scatter(
        net, 4, y,
        lambda i: buf.at[x, i, z, sc],
        lambda i: buf.at[x, i, z, sz(ra + rb, hc)],
        lambda i: buf.at[x, i, z, sz(ra + rb + hc, rc - hc)],
        slots[6], yr, yl)

    def gate_ring():
        xo = 2 - 2 * (x // 2)
        c = net.send(ggd.at[sz(xo, 2)], gg_rx.at[sz(0, 2)], x_far)
        yield
        c.wait_recv()
        xm = 2 * (x // 2)
        for k in range(2):
            for j in range(4):
                ggd[xm + k, j] = ggd[xm + k, j] + gg_rx[k, j]
        xn = x + 1 - 2 * lax.rem(x, 2)
        c = net.send(ggd.at[xn], gg_rx.at[2], x_near)
        yield
        c.wait_recv()
        for j in range(4):
            ggd[x, j] = ggd[x, j] + gg_rx[2, j]
        yo = 2 - 2 * (y // 2)
        c = net.send(ggd.at[x, sz(yo, 2)], gg_rx.at[3, sz(0, 2)], y_far)
        yield
        c.wait_recv()
        ym = 2 * (y // 2)
        for k in range(2):
            ggd[x, ym + k] = ggd[x, ym + k] + gg_rx[3, k]
        yn = y + 1 - 2 * lax.rem(y, 2)
        c = net.send(ggd.at[x, yn], gg_rx.at[3, 2], y_near)
        yield
        c.wait_recv()
        gg_rz[0] = ggd[x, y] + gg_rx[3, 2]
        for k, d in enumerate((z1, z2, z4)):
            c = net.send(gg_rz.at[2 * k], gg_rz.at[2 * k + 1], d)
            yield
            c.wait_recv()
            gg_rz[2 * k + 2] = gg_rz[2 * k] + gg_rz[2 * k + 1]
        yield

    def launch(k):
        for zz in stage[k]:
            produce(zz)
        step(back[k])

    tn = (((0,), (0,)), ((), ()))

    def other_grads(j):
        e = 2 * (1 - core) + j

        def body(h, _):
            for q in range(2):
                m = 2 * h + q
                f = pl.ds(pl.multiple_of(m * W, W), W)
                osg[j, f, :] = lax.dot_general(xs[m, e], pgu[e], tn, preferred_element_type=F32).astype(BF)
                osd[j, :, f] = lax.dot_general(sh[e], gxs[m, e], tn, preferred_element_type=F32).astype(BF)
            return 0

        if COMPUTE:
            lax.fori_loop(0, NZ // 2, body, 0)
        return [net.send(osg.at[j], org.at[j], sibling), net.send(osd.at[j], ord_.at[j], sibling)]

    def own_grads(lo, hi):
        def outs(j, m, slot):
            f = pl.ds(pl.multiple_of(m * W, W), W)
            return [
                pltpu.make_async_copy(stg.at[slot], dgu_out.at[j, f, :], stg_sem.at[slot, 0]),
                pltpu.make_async_copy(std.at[slot], dd_out.at[j, :, f], stg_sem.at[slot, 1]),
            ]

        def body(t, _):
            for slot in range(2):
                j, m = t // (NZ // 2), 2 * (t % (NZ // 2)) + slot
                e = 2 * core + j
                f = pl.ds(pl.multiple_of(m * W, W), W)

                @pl.when(t >= 1)
                def _():
                    for c in outs(j, m, slot):
                        c.wait()

                a = lax.dot_general(xs[m, e], pgu[e], tn, preferred_element_type=F32)
                stg[slot] = (a + org[j, f, :].astype(F32)).astype(BF)
                b = lax.dot_general(sh[e], gxs[m, e], tn, preferred_element_type=F32)
                std[slot] = (b + ord_[j, :, f].astype(F32)).astype(BF)
                for c in outs(j, m, slot):
                    c.start()
            return 0

        if COMPUTE:
            lax.fori_loop(lo, hi, body, 0)
            if hi == NZ:
                for slot in range(2):
                    for c in outs(0, 0, slot):
                        c.wait()

    ring = gate_ring()
    launch(4)
    run(sza)
    launch(3)
    step(back[4])
    run(sza)
    launch(2)
    step(back[4])
    run(szb, szc)
    step(back[3])
    if COMPUTE:
        loop(PAIRS, gate_terms)
    run(ring)
    launch(1)
    step(back[3])
    run(szb, szc, sza)
    step(back[2])
    run(ring)
    launch(0)
    grad_copies = other_grads(0)
    step(back[2])
    run(szb, szc, sza)
    step(back[1])
    run(ring)
    grad_copies += other_grads(1)
    run(ring)
    step(back[1])
    run(szb, szc, sza)
    run(sya)
    step(back[0])
    run(ring)
    step(back[0])
    for c in grad_copies:
        c.wait_recv()
    own_grads(0, 3)
    run(szb, szc)
    run(sxb, syc)
    run(sya, ring)
    own_grads(3, 5)
    run(sya)
    run(sxa, sxb, syc)
    own_grads(5, 7)
    run(ring, sxa, sxb, syc)
    run(ring)
    own_grads(7, 8)
    run(sxa)

    tok_out[...] = buf[x, y, z, 0:TOK, :]
    gg_out[...] = gg_rz[6]
    net.drain()


def finish_kernel(tok, gg, dgu, dd, tok_out, gg_out, dg_out, du_out, dd_out):
    tok_out[...] = tok[...]
    gg_out[...] = gg[...]
    dg_out[...] = dgu[:, :, :H].astype(F32)
    du_out[...] = dgu[:, :, H:].astype(F32)
    dd_out[...] = dd[...].astype(F32)


def finish(tok, gg, dgu, dd):
    steps = 4
    n = D // steps
    whole = lambda i: (0, 0)
    rows = lambda i: (0, i, 0)
    cols = lambda i: (0, 0, i)
    return pl.pallas_call(
        finish_kernel,
        grid=(steps,),
        in_specs=[
            pl.BlockSpec((TOK, W), whole),
            pl.BlockSpec((8, TOK), whole),
            pl.BlockSpec((2, n, 2 * H), rows),
            pl.BlockSpec((2, H, n), cols),
        ],
        out_specs=[
            pl.BlockSpec((TOK, W), whole),
            pl.BlockSpec((8, TOK), whole),
            pl.BlockSpec((2, n, H), rows),
            pl.BlockSpec((2, n, H), rows),
            pl.BlockSpec((2, H, n), cols),
        ],
        out_shape=(
            jax.ShapeDtypeStruct((TOK, W), BF),
            jax.ShapeDtypeStruct((8, TOK), F32),
            jax.ShapeDtypeStruct((2, D, H), F32),
            jax.ShapeDtypeStruct((2, D, H), F32),
            jax.ShapeDtypeStruct((2, H, D), F32),
        ),
        compiler_params=pltpu.CompilerParams(vmem_limit_bytes=62 * 1024 * 1024),
    )(tok, gg, dgu, dd)


def local(tokens, grad_output, gates, ids, gate_weight, up_weight, down_weight):
    any_spec = pl.BlockSpec(memory_space=pl.ANY)
    vmem = pl.BlockSpec(memory_space=pltpu.VMEM)
    scratch = [
        pltpu.VMEM((NX, NY, NZ, 2 * TOK, W), BF),
        pltpu.VMEM((NZ, E4, ROWS, W), BF),
        pltpu.VMEM((NZ, E4, ROWS, W), BF),
        pltpu.VMEM((E4, D, 2 * H), BF),
        pltpu.VMEM((E4, H, D), BF),
        pltpu.VMEM((PAIRS, 192, 2 * TOK), BF),
        pltpu.VMEM((PAIRS, 2 * TOK, 192), BF),
        pltpu.VMEM((PAIRS, 192, W), BF),
        pltpu.VMEM((E4, ROWS, 2 * H), F32),
        pltpu.VMEM((E4, ROWS, H), F32),
        pltpu.VMEM((E4, ROWS, 2 * H), BF),
        pltpu.VMEM((E4, ROWS, H), BF),
        pltpu.VMEM((E4, ROWS, H), F32),
        pltpu.VMEM((64, TOK), F32),
        pltpu.VMEM((64, TOK), F32),
        pltpu.VMEM((64, TOK), F32),
        pltpu.VMEM((NX, NY, 16, TOK), F32),
        pltpu.VMEM((NX, NY, 8, TOK), F32),
        pltpu.VMEM((4, 4, 8, TOK), F32),
        pltpu.VMEM((7, 8, TOK), F32),
        pltpu.VMEM((2, D, 2 * H), BF),
        pltpu.VMEM((2, H, D), BF),
        pltpu.VMEM((2, D, 2 * H), BF),
        pltpu.VMEM((2, H, D), BF),
        pltpu.VMEM((2, W, 2 * H), BF),
        pltpu.VMEM((2, H, W), BF),
    ]
    for ring in scatter_slots():
        for pair in ring:
            for shape in pair:
                scratch.append(pltpu.VMEM(shape, BF))
    scratch += [
        pltpu.SemaphoreType.DMA((N_SEM,)),
        pltpu.SemaphoreType.DMA((N_SEM,)),
        pltpu.SemaphoreType.DMA((N_LOC,)),
        pltpu.SemaphoreType.DMA((2, 2)),
    ]
    outs = pl.pallas_call(
        kernel,
        out_shape=(
            jax.ShapeDtypeStruct((TOK, W), BF),
            jax.ShapeDtypeStruct((8, TOK), F32),
            jax.ShapeDtypeStruct((2, D, 2 * H), BF),
            jax.ShapeDtypeStruct((2, H, D), BF),
        ),
        in_specs=[any_spec, any_spec, vmem, vmem, any_spec, any_spec, any_spec],
        out_specs=(vmem, vmem, any_spec, any_spec),
        scratch_shapes=scratch,
        compiler_params=pltpu.CompilerParams(
            collective_id=0, has_side_effects=True, vmem_limit_bytes=63 * 1024 * 1024
        ),
    )(tokens, grad_output, ids.T, gates.T, gate_weight, up_weight, down_weight)
    grad_tokens, gate_grads, grad_gate, grad_up, grad_down = finish(*outs)
    return (grad_tokens, gate_grads.T, grad_gate, grad_up, grad_down)


def solution(mesh):
    return jax.shard_map(
        local,
        mesh=mesh,
        in_specs=(
            P("expert", "etp"),
            P("expert", "etp"),
            P("expert", None),
            P("expert", None),
            P("expert", None, "etp"),
            P("expert", None, "etp"),
            P("expert", "etp", None),
        ),
        out_specs=(
            P("expert", "etp"),
            P("expert", None),
            P("expert", None, "etp"),
            P("expert", None, "etp"),
            P("expert", "etp", None),
        ),
        check_vma=False,
    )
```

time: 196 us -> 160 us (0.82)
  Pallas kernels: 183 us -> 158 us
  local copies, waits for them, and re-layouts: 9.59 us -> 0 us
  other arithmetic: 1.98 us -> 0 us
    pallas_call x1, Pallas kernels: 183 us -> 153 us  [local(): pl.pallas_call(kernel, out_shape=(jax.ShapeDtypeStruct((TOK, W), BF), jax...]
    unnamed x9 -> x0, local copies, waits for them, and re-layouts: 9.59 us -> none
    pallas_call x0 -> x1, Pallas kernels: none -> 5.03 us  [finish(): pl.pallas_call(finish_kernel, grid=(steps,), in_specs=[pl.BlockSpec((TOK,...]
where the time goes in v2:
time: 160 us; the launch traced here: 159 us
  Pallas kernels  158 us (99%)
    pallas_call x1, Pallas kernels, local(): pl.pallas_call(kernel, out_shape=(jax.ShapeDtypeStruct((TOK, W), BF), jax...  153 us
    pallas_call x1, Pallas kernels, finish(): pl.pallas_call(finish_kernel, grid=(steps,), in_specs=[pl.BlockSpec((TOK,...  5.03 us

profile of v2, /device:TPU:32, one launch (start us, length us, event | category | flops | bytes accessed | tf_op | source)
XLA Modules:
  0.0 158.9 jit_solution(14163230753378797643)
XLA Ops:
  0.6 153.2 %shard_map.110 = (bf16[128,256]{1,0:T(8,128)(2,1)}, f32[8,128]{1,0:T(8,128)}, bf16[2,2048,256]{2,1,0:T(8,128)(2,1)}, bf16[2,128,2048]{2,1,0:T(8,128)(2,1)}) custom-call(bf16[128,256]{1,0:T(8,128)(2,1)} %refs_0_.1, bf16[128,256]{1,0:T(8,128)(2,1)} %refs_1_.1, s32[8,128]{1,0:T(8,128)} %bitcast.3, bf16[8,128]{1,0:T(8,128)(2,1)} %bitcast.4, ...), custom_call_target="tpu_custom_call" | custom-call | tf_op jit(solution)/shard_map/pallas_call | solution.py:743
  153.9 5.0 %shard_map.111 = (bf16[128,256]{1,0:T(8,128)(2,1)}, f32[8,128]{1,0:T(8,128)}, f32[2,2048,128]{2,1,0:T(8,128)}, f32[2,2048,128]{2,1,0:T(8,128)}, f32[2,128,2048]{2,1,0:T(8,128)}) custom-call(bf16[128,256]{1,0:T(8,128)(2,1)} %get-tuple-element.14.tok, f32[8,128]{1,0:T(8,128)} %get-tuple-element.15.gg, bf16[2,2048,256]{2,1,0:T(8,128)(2,1)} %get-tuple-element.16.dgu, ...), custom_call_target="tpu_custom_call" | custom-call | tf_op jit(solution)/shard_map/pallas_call | solution.py:675

commit v3 on v2

--- a/solution.py
+++ b/solution.py
@@ -22,7 +22,28 @@
 ROWS = 2 * CAP * PAIRS
 SPLIT_G = (48, 96, 112)
 SPLIT_R = (32, 48, 48)
-COMPUTE = True
+
+GATHER = (
+    "xab", "yc", "zb0", "zc0", "wl", "rt", "zb0", "yc", "xab", "zb1", "zb2", "zc1", "zc2", "rt", "zc0", "-16", "wl",
+    "yc", "zc3", "zb0", "xab", "zb3", "ya", "px0", "py0", "rt", "-7", "zb1", "zb2", "zc1", "-5", "zc2", "ya", "zc0",
+    "-4", "zc3", "px1", "px2", "-8", "px0", "zb0", "rt", "-5", "py0", "zb3", "py1", "py2", "ya", "za", "zb1", "zb2",
+    "-4", "zc1", "-4", "py0", "zc2", "px1", "-6", "zc0", "zc3", "px3", "px4", "zb0", "py1", "zb3", "py3", "py4",
+    "px2", "px0", "py2", "-15", "rt", "route", "pick0", "py1", "acc0", "px1", "-4", "za", "pick1", "zb1", "acc1",
+    "zb2", "py3", "-8", "zc1", "px3", "zc2", "-6", "zc0", "py4", "zc3", "px5", "px6", "zb3", "py5", "py6", "-8",
+    "py2", "px4", "py3", "-6", "px2", "pick2", "py4", "acc2", "px3", "za", "pick3", "zb1", "zb2", "py5", "zc1",
+    "acc3", "zc2", "-8", "zc3", "px5", "px7", "zb3", "py7", "-12", "py6", "py5", "-8", "px6", "px4", "pick4", "py7",
+    "acc4", "za", "px5", "pick5", "py6", "acc5", "-8", "py7", "-6", "px7", "za", "-6", "px6", "pick6", "acc6",
+    "px7", "pick7", "acc7",
+)
+SCATTER = (
+    "make7", "sza", "rx7", "ry7", "make6", "rx6", "ry6", "make5", "rx7", "rx5", "ry7", "ry5", "make4", "sza", "rx6",
+    "rx4", "ry6", "ry4", "make3", "rx7", "szc", "rx3", "ry7", "szb", "ry3", "make2", "rx5", "rx2", "ry5", "ry2",
+    "rx6", "make1", "rx4", "rx1", "rx3", "ry6", "ry4", "ry3", "sza", "ry1", "make0", "rx5", "szc", "rx0", "ry5",
+    "szb", "rx2", "ry2", "ry0", "gt", "rx4", "rx1", "ry4", "gr", "og0", "sza", "rx3", "rx0", "ry3", "ry1", "og1",
+    "szc", "szb", "rx2", "ry2", "ry0", "-8", "rx1", "-16", "gr", "ry1", "-48", "wg0", "rx0", "gr", "wg1", "ry0",
+    "wg2", "sza", "sya", "wg3", "wg4", "gr", "wg5", "szc", "wg6", "sya", "wg7", "gr", "szb", "-23", "gr", "szc",
+    "sya", "syc", "sxa", "-6", "szb", "sxb", "gr", "-5", "sxa", "syc", "gr", "sxb", "-7", "sxa", "syc", "sxb",
+)
 
 
 class Net:
@@ -46,10 +67,11 @@
         self.pending.append(copy)
         return copy
 
-    def drain(self):
-        for copy in self.pending:
+    def drain(self, n=None):
+        n = len(self.pending) if n is None else n
+        for copy in self.pending[:n]:
             copy.wait_send()
-        self.pending = []
+        self.pending = self.pending[n:]
 
 
 def half16(n):
@@ -59,22 +81,22 @@
 def ring4_gather(net, i, full, h0, h1, right, left):
     a = net.send(full(i), full(i), right)
     b = net.send(full(i), full(i), left)
-    yield
+    yield a, b
     prev, following = lax.rem(i + 3, 4), lax.rem(i + 1, 4)
     a.wait_recv()
     c = net.send(h0(prev), h0(prev), right)
     b.wait_recv()
     d = net.send(h1(following), h1(following), left)
-    yield
+    yield c, d
     c.wait_recv()
     d.wait_recv()
-    yield
+    yield ()
 
 
 def ring8_gather(net, i, full, h0, h1, right, left):
     a = net.send(full(i), full(i), right)
     b = net.send(full(i), full(i), left)
-    yield
+    yield a, b
     for step in (1, 2, 3):
         prev, following = lax.rem(i + 8 - step, 8), lax.rem(i + step, 8)
         va, vb = (full, full) if step < 3 else (h0, h1)
@@ -82,10 +104,10 @@
         a = net.send(va(prev), va(prev), right)
         b.wait_recv()
         b = net.send(vb(following), vb(following), left)
-        yield
+        yield a, b
     a.wait_recv()
     b.wait_recv()
-    yield
+    yield ()
 
 
 def add_into(dst, src):
@@ -97,7 +119,7 @@
     ra, rb = slots[0]
     a = net.send(h0(far), ra, right)
     b = net.send(h1(far), rb, left)
-    yield
+    yield a, b
     for step in range(1, n // 2):
         to_r, to_l = lax.rem(i + n // 2 - step, n), lax.rem(i + n // 2 + step, n)
         va, vb = (h0, h1) if step == 1 else (full, full)
@@ -109,17 +131,12 @@
         add_into(vb(to_l), rb)
         rb = rb_next
         b = net.send(full(to_l), rb, left)
-        yield
+        yield a, b
     a.wait_recv()
     b.wait_recv()
     dst = full(i)
     dst[...] = (dst[...].astype(F32) + ra[...].astype(F32) + rb[...].astype(F32)).astype(BF)
-    yield
-
-
-def run(*gens):
-    for g in gens:
-        next(g)
+    yield ()
 
 
 def scatter_slots():
@@ -210,7 +227,7 @@
     sz = pl.ds
     ra, rb, rc = SPLIT_G
     ga, gb, gab, gc = sz(0, ra), sz(ra, rb), sz(0, ra + rb), sz(ra + rb, rc)
-    hab, hc = half16(ra + rb), half16(rc)
+    hab, hb, hc = half16(ra + rb), half16(rb), half16(rc)
     zs = [z] + [lax.rem(z + k + 8, 8) for k in (1, -1, 2, -2, 3, -3, 4)]
     stage = [zs[0:1], zs[1:3], zs[3:5], zs[5:7], zs[7:8]]
 
@@ -238,18 +255,21 @@
         lambda i: buf.at[sz(0, 2), :, i, ga],
         lambda i: buf.at[sz(2, 2), :, i, ga],
         zr, zl)
-    zb = ring8_gather(
-        net, z,
-        lambda i: buf.at[:, y, i, gb],
-        lambda i: buf.at[sz(0, 2), y, i, gb],
-        lambda i: buf.at[sz(2, 2), y, i, gb],
-        zr, zl)
-    zc = ring8_gather(
-        net, z,
-        lambda i: buf.at[x, :, i, gc],
-        lambda i: buf.at[x, sz(0, 2), i, gc],
-        lambda i: buf.at[x, sz(2, 2), i, gc],
-        zr, zl)
+    def column_b(px):
+        return ring8_gather(
+            net, z,
+            lambda i: buf.at[px, y, i, gb],
+            lambda i: buf.at[px, y, i, sz(ra, hb)],
+            lambda i: buf.at[px, y, i, sz(ra + hb, rb - hb)],
+            zr, zl)
+
+    def column_c(py):
+        return ring8_gather(
+            net, z,
+            lambda i: buf.at[x, py, i, gc],
+            lambda i: buf.at[x, py, i, sz(ra + rb, hc)],
+            lambda i: buf.at[x, py, i, sz(ra + rb + hc, rc - hc)],
+            zr, zl)
 
     def plane(zz):
         return (
@@ -267,47 +287,54 @@
                 yr, yl),
         )
 
-    planes = [[plane(zz) for zz in group] for group in stage]
-
-    def step(groups):
-        for pair in groups:
-            run(*pair)
-
     def route_ring():
         c = net.send(rt.at[x, y], rt.at[x, y], y_near)
-        yield
+        yield (c,)
         c.wait_recv()
         yh = 2 * (y // 2)
         c = net.send(rt.at[x, sz(yh, 2)], rt.at[x, sz(yh, 2)], y_far)
-        yield
+        yield (c,)
         c.wait_recv()
         c = net.send(rt.at[x], rt.at[x], x_near)
-        yield
+        yield (c,)
         c.wait_recv()
         xh = 2 * (x // 2)
         c = net.send(rt.at[sz(xh, 2)], rt.at[sz(xh, 2)], x_far)
-        yield
+        yield (c,)
         c.wait_recv()
-        yield
-
-    routing = route_ring()
-    run(xab, yc, routing)
-    run(xab, yc, routing)
-    run(xab, yc)
-    run(ya, zb, zc)
-    step(planes[0])
-    run(routing, ya)
-    for c in own_copies[2:]:
-        c.wait()
-    weight_copies = []
-    for j in range(2):
-        ce = 2 * core + j
-        weight_copies.append(net.send(wgu.at[ce], wgu.at[ce], sibling))
-        weight_copies.append(net.send(wd.at[ce], wd.at[ce], sibling))
-    run(ya)
-    run(routing)
-    step(planes[0])
-    run(routing)
+        yield ()
+
+    def load_weights():
+        for c in own_copies[2:]:
+            c.wait()
+        copies = []
+        for j in range(2):
+            ce = 2 * core + j
+            copies.append(net.send(wgu.at[ce], wgu.at[ce], sibling))
+            copies.append(net.send(wd.at[ce], wd.at[ce], sibling))
+        yield copies
+        for c in copies:
+            c.wait_recv()
+        yield ()
+
+    tasks = {}
+
+    def ring_task(name, steps):
+        tasks[name] = lambda: next(steps)
+
+    ring_task("xab", xab)
+    ring_task("yc", yc)
+    ring_task("ya", ya)
+    ring_task("za", za)
+    for k, d in enumerate((0, 1, 3, 2)):
+        ring_task(f"zb{k}", column_b(lax.rem(x + d, 4)))
+        ring_task(f"zc{k}", column_c(lax.rem(y + d, 4)))
+    for k, zz in enumerate(zs):
+        gx, gy = plane(zz)
+        ring_task(f"px{k}", gx)
+        ring_task(f"py{k}", gy)
+    ring_task("rt", route_ring())
+    ring_task("wl", load_weights())
     first_expert = 4 * (x * 4 + y)
 
     def route():
@@ -367,12 +394,6 @@
 
         for e in range(E4):
             body(e)
-
-    def consume(group, first=False):
-        if COMPUTE:
-            for zz in group:
-                pick(zz)
-                accumulate(zz, first)
 
     def forward(e):
         gu, raw = agu[e], araw[e]
@@ -408,10 +429,9 @@
                 buf[2 * p + q // 2, 2 * (q % 2) : 2 * (q % 2) + 2, zz, 0:TOK, :] = o.reshape(2, TOK, W)
             return 0
 
-        if COMPUTE:
-            for e in range(E4):
-                products(e)
-            lax.fori_loop(0, PAIRS // 4, spread, 0)
+        for e in range(E4):
+            products(e)
+        lax.fori_loop(0, PAIRS // 4, spread, 0)
 
     def gate_terms(p):
         for k in range(2):
@@ -432,23 +452,20 @@
 
         lax.fori_loop(0, n, body, 0)
 
-    if COMPUTE:
-        route()
-    for c in weight_copies:
-        c.wait_recv()
-    for k in range(1, 5):
-        run(zb, zc)
-        step(planes[k])
-        step(planes[k - 1])
-        run(za)
-        consume(stage[k - 1], k == 1)
-        step(planes[k])
-    step(planes[4])
-    run(za)
-    consume(stage[4])
+    def do(order):
+        for name in order:
+            if name[0] == "-":
+                net.drain(int(name[1:]))
+            else:
+                tasks[name]()
+
+    tasks["route"] = route
+    for k, zz in enumerate(zs):
+        tasks[f"pick{k}"] = functools.partial(pick, zz)
+        tasks[f"acc{k}"] = functools.partial(accumulate, zz, k == 0)
+    do(GATHER)
     net.drain()
-    if COMPUTE:
-        loop(E4, forward)
+    loop(E4, forward)
 
     ra, rb, rc = SPLIT_R
     sa, sb, sc = sz(0, ra), sz(ra, rb), sz(ra + rb, rc)
@@ -470,8 +487,11 @@
                 slots[2 * k + 1], yr, yl),
         )
 
-    back = [rplane(k, zz) for k, zz in enumerate(zs)]
-    back = [back[0:1], back[1:3], back[3:5], back[5:7], back[7:8]]
+    for k, zz in enumerate(zs):
+        gx, gy = rplane(k, zz)
+        ring_task(f"rx{k}", gx)
+        ring_task(f"ry{k}", gy)
+        tasks[f"make{k}"] = functools.partial(produce, zz)
     slots = slots[16:]
     sza = ring_scatter(
         net, 8, z,
@@ -519,7 +539,7 @@
     def gate_ring():
         xo = 2 - 2 * (x // 2)
         c = net.send(ggd.at[sz(xo, 2)], gg_rx.at[sz(0, 2)], x_far)
-        yield
+        yield (c,)
         c.wait_recv()
         xm = 2 * (x // 2)
         for k in range(2):
@@ -527,35 +547,32 @@
                 ggd[xm + k, j] = ggd[xm + k, j] + gg_rx[k, j]
         xn = x + 1 - 2 * lax.rem(x, 2)
         c = net.send(ggd.at[xn], gg_rx.at[2], x_near)
-        yield
+        yield (c,)
         c.wait_recv()
         for j in range(4):
             ggd[x, j] = ggd[x, j] + gg_rx[2, j]
         yo = 2 - 2 * (y // 2)
         c = net.send(ggd.at[x, sz(yo, 2)], gg_rx.at[3, sz(0, 2)], y_far)
-        yield
+        yield (c,)
         c.wait_recv()
         ym = 2 * (y // 2)
         for k in range(2):
             ggd[x, ym + k] = ggd[x, ym + k] + gg_rx[3, k]
         yn = y + 1 - 2 * lax.rem(y, 2)
         c = net.send(ggd.at[x, yn], gg_rx.at[3, 2], y_near)
-        yield
+        yield (c,)
         c.wait_recv()
         gg_rz[0] = ggd[x, y] + gg_rx[3, 2]
         for k, d in enumerate((z1, z2, z4)):
             c = net.send(gg_rz.at[2 * k], gg_rz.at[2 * k + 1], d)
-            yield
+            yield (c,)
             c.wait_recv()
             gg_rz[2 * k + 2] = gg_rz[2 * k] + gg_rz[2 * k + 1]
-        yield
-
-    def launch(k):
-        for zz in stage[k]:
-            produce(zz)
-        step(back[k])
+        yield ()
 
     tn = (((0,), (0,)), ((), ()))
+
+    grad_copies = []
 
     def other_grads(j):
         e = 2 * (1 - core) + j
@@ -568,9 +585,8 @@
                 osd[j, :, f] = lax.dot_general(sh[e], gxs[m, e], tn, preferred_element_type=F32).astype(BF)
             return 0
 
-        if COMPUTE:
-            lax.fori_loop(0, NZ // 2, body, 0)
-        return [net.send(osg.at[j], org.at[j], sibling), net.send(osd.at[j], ord_.at[j], sibling)]
+        lax.fori_loop(0, NZ // 2, body, 0)
+        grad_copies.extend([net.send(osg.at[j], org.at[j], sibling), net.send(osd.at[j], ord_.at[j], sibling)])
 
     def own_grads(lo, hi):
         def outs(j, m, slot):
@@ -599,59 +615,24 @@
                     c.start()
             return 0
 
-        if COMPUTE:
-            lax.fori_loop(lo, hi, body, 0)
-            if hi == NZ:
-                for slot in range(2):
-                    for c in outs(0, 0, slot):
-                        c.wait()
-
-    ring = gate_ring()
-    launch(4)
-    run(sza)
-    launch(3)
-    step(back[4])
-    run(sza)
-    launch(2)
-    step(back[4])
-    run(szb, szc)
-    step(back[3])
-    if COMPUTE:
-        loop(PAIRS, gate_terms)
-    run(ring)
-    launch(1)
-    step(back[3])
-    run(szb, szc, sza)
-    step(back[2])
-    run(ring)
-    launch(0)
-    grad_copies = other_grads(0)
-    step(back[2])
-    run(szb, szc, sza)
-    step(back[1])
-    run(ring)
-    grad_copies += other_grads(1)
-    run(ring)
-    step(back[1])
-    run(szb, szc, sza)
-    run(sya)
-    step(back[0])
-    run(ring)
-    step(back[0])
-    for c in grad_copies:
-        c.wait_recv()
-    own_grads(0, 3)
-    run(szb, szc)
-    run(sxb, syc)
-    run(sya, ring)
-    own_grads(3, 5)
-    run(sya)
-    run(sxa, sxb, syc)
-    own_grads(5, 7)
-    run(ring, sxa, sxb, syc)
-    run(ring)
-    own_grads(7, 8)
-    run(sxa)
+        if lo == 0:
+            for c in grad_copies:
+                c.wait_recv()
+        lax.fori_loop(lo, hi, body, 0)
+        if hi == NZ:
+            for slot in range(2):
+                for c in outs(0, 0, slot):
+                    c.wait()
+
+    for name, steps in (("sza", sza), ("szb", szb), ("szc", szc), ("sya", sya),
+                        ("sxa", sxa), ("sxb", sxb), ("syc", syc), ("gr", gate_ring())):
+        ring_task(name, steps)
+    tasks["gt"] = lambda: loop(PAIRS, gate_terms)
+    for j in range(2):
+        tasks[f"og{j}"] = functools.partial(other_grads, j)
+    for t in range(NZ):
+        tasks[f"wg{t}"] = functools.partial(own_grads, t, t + 1)
+    do(SCATTER)
 
     tok_out[...] = buf[x, y, z, 0:TOK, :]
     gg_out[...] = gg_rz[6]

time: 160 us -> 149 us (0.931)
  Pallas kernels: 158 us -> 147 us
    pallas_call x1, Pallas kernels: 153 us -> 142 us  [local(): pl.pallas_call(kernel, out_shape=(jax.ShapeDtypeStruct((TOK, W), BF), jax...]
where the time goes in v3:
time: 149 us; the launch traced here: 148 us
  Pallas kernels  147 us (99%)
    pallas_call x1, Pallas kernels, local(): pl.pallas_call(kernel, out_shape=(jax.ShapeDtypeStruct((TOK, W), BF), jax...  142 us
    pallas_call x1, Pallas kernels, finish(): pl.pallas_call(finish_kernel, grid=(steps,), in_specs=[pl.BlockSpec((TOK,...  5.03 us

profile of v3, /device:TPU:32, one launch (start us, length us, event | category | flops | bytes accessed | tf_op | source)
XLA Modules:
  0.0 148.0 jit_solution(7155914362122748372)
XLA Ops:
  0.6 142.3 %shard_map.110 = (bf16[128,256]{1,0:T(8,128)(2,1)}, f32[8,128]{1,0:T(8,128)}, bf16[2,2048,256]{2,1,0:T(8,128)(2,1)}, bf16[2,128,2048]{2,1,0:T(8,128)(2,1)}) custom-call(bf16[128,256]{1,0:T(8,128)(2,1)} %refs_0_.1, bf16[128,256]{1,0:T(8,128)(2,1)} %refs_1_.1, s32[8,128]{1,0:T(8,128)} %bitcast.3, bf16[8,128]{1,0:T(8,128)(2,1)} %bitcast.4, ...), custom_call_target="tpu_custom_call" | custom-call | tf_op jit(solution)/shard_map/pallas_call | solution.py:724
  143.0 5.0 %shard_map.111 = (bf16[128,256]{1,0:T(8,128)(2,1)}, f32[8,128]{1,0:T(8,128)}, f32[2,2048,128]{2,1,0:T(8,128)}, f32[2,2048,128]{2,1,0:T(8,128)}, f32[2,128,2048]{2,1,0:T(8,128)}) custom-call(bf16[128,256]{1,0:T(8,128)(2,1)} %get-tuple-element.14.tok, f32[8,128]{1,0:T(8,128)} %get-tuple-element.15.gg, bf16[2,2048,256]{2,1,0:T(8,128)(2,1)} %get-tuple-element.16.dgu, ...), custom_call_target="tpu_custom_call" | custom-call | tf_op jit(solution)/shard_map/pallas_call | solution.py:656

commit v4 on v3

--- a/solution.py
+++ b/solution.py
@@ -24,25 +24,25 @@
 SPLIT_R = (32, 48, 48)
 
 GATHER = (
-    "xab", "yc", "zb0", "zc0", "wl", "rt", "zb0", "yc", "xab", "zb1", "zb2", "zc1", "zc2", "rt", "zc0", "-16", "wl",
-    "yc", "zc3", "zb0", "xab", "zb3", "ya", "px0", "py0", "rt", "-7", "zb1", "zb2", "zc1", "-5", "zc2", "ya", "zc0",
-    "-4", "zc3", "px1", "px2", "-8", "px0", "zb0", "rt", "-5", "py0", "zb3", "py1", "py2", "ya", "za", "zb1", "zb2",
-    "-4", "zc1", "-4", "py0", "zc2", "px1", "-6", "zc0", "zc3", "px3", "px4", "zb0", "py1", "zb3", "py3", "py4",
-    "px2", "px0", "py2", "-15", "rt", "route", "pick0", "py1", "acc0", "px1", "-4", "za", "pick1", "zb1", "acc1",
-    "zb2", "py3", "-8", "zc1", "px3", "zc2", "-6", "zc0", "py4", "zc3", "px5", "px6", "zb3", "py5", "py6", "-8",
-    "py2", "px4", "py3", "-6", "px2", "pick2", "py4", "acc2", "px3", "za", "pick3", "zb1", "zb2", "py5", "zc1",
-    "acc3", "zc2", "-8", "zc3", "px5", "px7", "zb3", "py7", "-12", "py6", "py5", "-8", "px6", "px4", "pick4", "py7",
-    "acc4", "za", "px5", "pick5", "py6", "acc5", "-8", "py7", "-6", "px7", "za", "-6", "px6", "pick6", "acc6",
-    "px7", "pick7", "acc7",
+    "yc", "zb0", "wl", "zc0", "xab", "rt", "yc", "zb0", "zc1", "zc2", "-8", "yc", "px0", "zc3", "zc0", "xab", "zb2",
+    "zb1", "wl", "rt", "xab", "zb3", "ya", "py0", "zb0", "-13", "zc1", "rt", "zc2", "zc3", "px1", "ya", "px2", "-8",
+    "px0", "zc0", "rt", "zb2", "ya", "-8", "zb1", "zb3", "za", "py2", "py1", "zb0", "-8", "py0", "zc1", "-5", "px1",
+    "zc2", "zc3", "px4", "px3", "zc0", "zb2", "py2", "zb1", "px2", "zb3", "py4", "py3", "-13", "px0", "py1", "rt",
+    "route", "py0", "pick0", "px1", "acc0", "-6", "py2", "za", "zb0", "-8", "zc1", "px4", "py4", "-6", "zc2", "zc3",
+    "px5", "px6", "zc0", "-8", "zb2", "py3", "zb1", "px3", "-8", "zb3", "py5", "py6", "py1", "pick1", "px2",
+    "pick2", "py4", "acc1", "acc2", "px4", "-4", "py3", "za", "px5", "zc1", "pick4", "zc2", "py5", "zc3", "px8",
+    "px7", "zb2", "acc4", "zb1", "zb3", "py8", "py7", "-16", "py6", "px6", "-14", "py5", "px3", "pick3", "acc3",
+    "py8", "px5", "-6", "py7", "za", "pick5", "px8", "py6", "acc5", "py8", "-8", "px7", "py7", "-8", "px6", "pick6",
+    "acc6", "px8", "za", "-6", "px7", "pick7", "acc7",
 )
 SCATTER = (
-    "make7", "sza", "rx7", "ry7", "make6", "rx6", "ry6", "make5", "rx7", "rx5", "ry7", "ry5", "make4", "sza", "rx6",
-    "rx4", "ry6", "ry4", "make3", "rx7", "szc", "rx3", "ry7", "szb", "ry3", "make2", "rx5", "rx2", "ry5", "ry2",
-    "rx6", "make1", "rx4", "rx1", "rx3", "ry6", "ry4", "ry3", "sza", "ry1", "make0", "rx5", "szc", "rx0", "ry5",
-    "szb", "rx2", "ry2", "ry0", "gt", "rx4", "rx1", "ry4", "gr", "og0", "sza", "rx3", "rx0", "ry3", "ry1", "og1",
-    "szc", "szb", "rx2", "ry2", "ry0", "-8", "rx1", "-16", "gr", "ry1", "-48", "wg0", "rx0", "gr", "wg1", "ry0",
-    "wg2", "sza", "sya", "wg3", "wg4", "gr", "wg5", "szc", "wg6", "sya", "wg7", "gr", "szb", "-23", "gr", "szc",
-    "sya", "syc", "sxa", "-6", "szb", "sxb", "gr", "-5", "sxa", "syc", "gr", "sxb", "-7", "sxa", "syc", "sxb",
+    "make7", "sza", "ry7", "rx7", "make6", "ry6", "rx6", "make5", "sza", "ry5", "rx5", "make4", "ry7", "ry4", "rx7",
+    "rx4", "make3", "sza", "ry6", "ry5", "ry3", "rx6", "rx5", "rx3", "make2", "ry2", "rx2", "ry7", "szb", "make1",
+    "ry4", "ry1", "rx7", "szc", "rx4", "rx1", "sza", "make0", "ry6", "ry0", "rx6", "rx0", "gt", "ry5", "szb", "ry3",
+    "ry2", "gr", "rx5", "szc", "rx3", "rx2", "og0", "sza", "ry4", "ry1", "ry0", "gr", "rx4", "rx1", "ry3", "szb",
+    "rx0", "og1", "ry2", "gr", "rx3", "szc", "ry1", "rx2", "-16", "rx1", "-8", "ry0", "-8", "gr", "-8", "sza",
+    "sya", "rx0", "wg0", "wg1", "wg2", "szb", "gr", "wg3", "wg4", "szc", "wg5", "wg6", "sya", "sxa", "wg7", "gr",
+    "szb", "sxb", "-32", "sxa", "szc", "syc", "gr", "-16", "sxb", "-24", "gr", "syc",
 )
 
 
@@ -90,6 +90,32 @@
     yield c, d
     c.wait_recv()
     d.wait_recv()
+    yield ()
+
+
+def direct_gather(net, i, full, right, left, far):
+    a = net.send(full(i), full(i), right)
+    b = net.send(full(i), full(i), left)
+    c = net.send(full(i), full(i), far)
+    yield a, b
+    a.wait_recv()
+    b.wait_recv()
+    yield (c,)
+    c.wait_recv()
+    yield ()
+
+
+def direct_scatter(net, i, full, slots, right, left, far):
+    prev, following, other = lax.rem(i + 3, 4), lax.rem(i + 1, 4), lax.rem(i + 2, 4)
+    a = net.send(full(other), slots[0][0], far)
+    b = net.send(full(following), slots[0][1], right)
+    c = net.send(full(prev), slots[1][0], left)
+    yield a, b, c
+    total = full(i)[...].astype(F32)
+    for copy, slot in ((b, slots[0][1]), (c, slots[1][0]), (a, slots[0][0])):
+        copy.wait_recv()
+        total = total + slot[...].astype(F32)
+    full(i)[...] = total.astype(BF)
     yield ()
 
 
@@ -114,23 +140,39 @@
     dst[...] = (dst[...].astype(F32) + src[...].astype(F32)).astype(BF)
 
 
-def ring_scatter(net, n, i, full, h0, h1, slots, right, left):
+def ring_scatter(net, n, i, full, h0, h1, slots, right, left, early=False):
     far = lax.rem(i + n // 2, n)
     ra, rb = slots[0]
     a = net.send(h0(far), ra, right)
     b = net.send(h1(far), rb, left)
-    yield a, b
+    yield () if early else (a, b)
+    if early:
+        to_r, to_l = lax.rem(far + n - 1, n), lax.rem(far + 1, n)
+        na, nb = slots[1]
+        a1 = net.send(h1(to_r), na.at[pl.ds(2, 2)], right)
+        b1 = net.send(h0(to_l), nb.at[pl.ds(0, 2)], left)
+        yield a, b
     for step in range(1, n // 2):
         to_r, to_l = lax.rem(i + n // 2 - step, n), lax.rem(i + n // 2 + step, n)
-        va, vb = (h0, h1) if step == 1 else (full, full)
+        halves = step == 1
+        if early and step == 2:
+            a1.wait_recv()
+            b1.wait_recv()
+        va, vb = (h0, h1) if halves else (full, full)
         a.wait_recv()
         add_into(va(to_r), ra)
         ra, rb_next = slots[step]
-        a = net.send(full(to_r), ra, right)
+        if early and halves:
+            a = net.send(h0(to_r), ra.at[pl.ds(0, 2)], right)
+        else:
+            a = net.send(full(to_r), ra, right)
         b.wait_recv()
         add_into(vb(to_l), rb)
         rb = rb_next
-        b = net.send(full(to_l), rb, left)
+        if early and halves:
+            b = net.send(h1(to_l), rb.at[pl.ds(2, 2)], left)
+        else:
+            b = net.send(full(to_l), rb, left)
         yield a, b
     a.wait_recv()
     b.wait_recv()
@@ -141,7 +183,6 @@
 
 def scatter_slots():
     ra, rb, rc = SPLIT_R
-    h = half16
     out = []
 
     def ring(n, half0, half1, whole):
@@ -153,10 +194,8 @@
     ring(8, (2, 4, ra, W), (2, 4, ra, W), (4, 4, ra, W))
     ring(8, (2, rb, W), (2, rb, W), (4, rb, W))
     ring(8, (2, rc, W), (2, rc, W), (4, rc, W))
-    ring(4, (2, ra, W), (2, ra, W), (4, ra, W))
-    ring(4, (h(ra), W), (ra - h(ra), W), (ra, W))
-    ring(4, (h(rb), W), (rb - h(rb), W), (rb, W))
-    ring(4, (h(rc), W), (rc - h(rc), W), (rc, W))
+    for shape in ((4, ra, W), (ra, W), (rb, W), (rc, W)):
+        out.append([(shape, shape), (shape,)])
     return out
 
 
@@ -174,7 +213,7 @@
     rt, ggd, gg_rx, gg_rz = take(4)
     osg, osd, org, ord_ = take(4)
     stg, std = take(2)
-    slots = [[tuple(take(2)) for _ in ring] for ring in scatter_slots()]
+    slots = [[tuple(take(len(pair))) for pair in ring] for ring in scatter_slots()]
     send_sem, recv_sem, loc_sem, stg_sem = take(4)
 
     e_idx = lax.axis_index("expert")
@@ -231,24 +270,9 @@
     zs = [z] + [lax.rem(z + k + 8, 8) for k in (1, -1, 2, -2, 3, -3, 4)]
     stage = [zs[0:1], zs[1:3], zs[3:5], zs[5:7], zs[7:8]]
 
-    xab = ring4_gather(
-        net, x,
-        lambda i: buf.at[i, y, z, gab],
-        lambda i: buf.at[i, y, z, sz(0, hab)],
-        lambda i: buf.at[i, y, z, sz(hab, ra + rb - hab)],
-        xr, xl)
-    yc = ring4_gather(
-        net, y,
-        lambda i: buf.at[x, i, z, gc],
-        lambda i: buf.at[x, i, z, sz(ra + rb, hc)],
-        lambda i: buf.at[x, i, z, sz(ra + rb + hc, rc - hc)],
-        yr, yl)
-    ya = ring4_gather(
-        net, y,
-        lambda i: buf.at[:, i, z, ga],
-        lambda i: buf.at[sz(0, 2), i, z, ga],
-        lambda i: buf.at[sz(2, 2), i, z, ga],
-        yr, yl)
+    xab = direct_gather(net, x, lambda i: buf.at[i, y, z, gab], xr, xl, x_far)
+    yc = direct_gather(net, y, lambda i: buf.at[x, i, z, gc], yr, yl, y_far)
+    ya = direct_gather(net, y, lambda i: buf.at[:, i, z, ga], yr, yl, y_far)
     za = ring8_gather(
         net, z,
         lambda i: buf.at[:, :, i, ga],
@@ -284,6 +308,23 @@
                 lambda i: buf.at[:, i, zz, gb],
                 lambda i: buf.at[sz(0, 2), i, zz, gb],
                 lambda i: buf.at[sz(2, 2), i, zz, gb],
+                yr, yl),
+        )
+
+    def half_plane(zz, k):
+        lo = 2 * k
+        return (
+            ring4_gather(
+                net, x,
+                lambda i: buf.at[i, sz(lo, 2), zz, gc],
+                lambda i: buf.at[i, sz(lo, 1), zz, gc],
+                lambda i: buf.at[i, sz(lo + 1, 1), zz, gc],
+                xr, xl),
+            ring4_gather(
+                net, y,
+                lambda i: buf.at[sz(lo, 2), i, zz, gb],
+                lambda i: buf.at[sz(lo, 1), i, zz, gb],
+                lambda i: buf.at[sz(lo + 1, 1), i, zz, gb],
                 yr, yl),
         )
 
@@ -330,9 +371,10 @@
         ring_task(f"zb{k}", column_b(lax.rem(x + d, 4)))
         ring_task(f"zc{k}", column_c(lax.rem(y + d, 4)))
     for k, zz in enumerate(zs):
-        gx, gy = plane(zz)
-        ring_task(f"px{k}", gx)
-        ring_task(f"py{k}", gy)
+        for h in range(1 + k // 7):
+            gx, gy = half_plane(zz, h) if k == 7 else plane(zz)
+            ring_task(f"px{k + h}", gx)
+            ring_task(f"py{k + h}", gy)
     ring_task("rt", route_ring())
     ring_task("wl", load_weights())
     first_expert = 4 * (x * 4 + y)
@@ -469,7 +511,6 @@
 
     ra, rb, rc = SPLIT_R
     sa, sb, sc = sz(0, ra), sz(ra, rb), sz(ra + rb, rc)
-    ha, hb, hc = half16(ra), half16(rb), half16(rc)
 
     def rplane(k, zz):
         return (
@@ -498,7 +539,7 @@
         lambda i: buf.at[:, :, i, sa],
         lambda i: buf.at[sz(0, 2), :, i, sa],
         lambda i: buf.at[sz(2, 2), :, i, sa],
-        slots[0], zr, zl)
+        slots[0], zr, zl, early=True)
     szb = ring_scatter(
         net, 8, z,
         lambda i: buf.at[:, y, i, sb],
@@ -511,30 +552,10 @@
         lambda i: buf.at[x, sz(0, 2), i, sc],
         lambda i: buf.at[x, sz(2, 2), i, sc],
         slots[2], zr, zl)
-    sya = ring_scatter(
-        net, 4, y,
-        lambda i: buf.at[:, i, z, sa],
-        lambda i: buf.at[sz(0, 2), i, z, sa],
-        lambda i: buf.at[sz(2, 2), i, z, sa],
-        slots[3], yr, yl)
-    sxa = ring_scatter(
-        net, 4, x,
-        lambda i: buf.at[i, y, z, sa],
-        lambda i: buf.at[i, y, z, sz(0, ha)],
-        lambda i: buf.at[i, y, z, sz(ha, ra - ha)],
-        slots[4], xr, xl)
-    sxb = ring_scatter(
-        net, 4, x,
-        lambda i: buf.at[i, y, z, sb],
-        lambda i: buf.at[i, y, z, sz(ra, hb)],
-        lambda i: buf.at[i, y, z, sz(ra + hb, rb - hb)],
-        slots[5], xr, xl)
-    syc = ring_scatter(
-        net, 4, y,
-        lambda i: buf.at[x, i, z, sc],
-        lambda i: buf.at[x, i, z, sz(ra + rb, hc)],
-        lambda i: buf.at[x, i, z, sz(ra + rb + hc, rc - hc)],
-        slots[6], yr, yl)
+    sya = direct_scatter(net, y, lambda i: buf.at[:, i, z, sa], slots[3], yr, yl, y_far)
+    sxa = direct_scatter(net, x, lambda i: buf.at[i, y, z, sa], slots[4], xr, xl, x_far)
+    sxb = direct_scatter(net, x, lambda i: buf.at[i, y, z, sb], slots[5], xr, xl, x_far)
+    syc = direct_scatter(net, y, lambda i: buf.at[x, i, z, sc], slots[6], yr, yl, y_far)
 
     def gate_ring():
         xo = 2 - 2 * (x // 2)

time: 149 us -> 139 us (0.933)
  Pallas kernels: 147 us -> 138 us
    pallas_call x1, Pallas kernels: 142 us -> 133 us  [local(): pl.pallas_call(kernel, out_shape=(jax.ShapeDtypeStruct((TOK, W), BF), jax...]
where the time goes in v4:
time: 139 us
  Pallas kernels  138 us (99%)
    pallas_call x1, Pallas kernels, local(): pl.pallas_call(kernel, out_shape=(jax.ShapeDtypeStruct((TOK, W), BF), jax...  133 us
    pallas_call x1, Pallas kernels, finish(): pl.pallas_call(finish_kernel, grid=(steps,), in_specs=[pl.BlockSpec((TOK,...  5.03 us

profile of v4, /device:TPU:32, one launch (start us, length us, event | category | flops | bytes accessed | tf_op | source)
XLA Modules:
  0.0 138.6 jit_solution(12928837595657459926)
XLA Ops:
  0.6 132.9 %shard_map.110 = (bf16[128,256]{1,0:T(8,128)(2,1)}, f32[8,128]{1,0:T(8,128)}, bf16[2,2048,256]{2,1,0:T(8,128)(2,1)}, bf16[2,128,2048]{2,1,0:T(8,128)(2,1)}) custom-call(bf16[128,256]{1,0:T(8,128)(2,1)} %refs_0_.1, bf16[128,256]{1,0:T(8,128)(2,1)} %refs_1_.1, s32[8,128]{1,0:T(8,128)} %bitcast.3, bf16[8,128]{1,0:T(8,128)(2,1)} %bitcast.4, ...), custom_call_target="tpu_custom_call" | custom-call | tf_op jit(solution)/shard_map/pallas_call | solution.py:745
  133.6 5.0 %shard_map.111 = (bf16[128,256]{1,0:T(8,128)(2,1)}, f32[8,128]{1,0:T(8,128)}, f32[2,2048,128]{2,1,0:T(8,128)}, f32[2,2048,128]{2,1,0:T(8,128)}, f32[2,128,2048]{2,1,0:T(8,128)}) custom-call(bf16[128,256]{1,0:T(8,128)(2,1)} %get-tuple-element.14.tok, f32[8,128]{1,0:T(8,128)} %get-tuple-element.15.gg, bf16[2,2048,256]{2,1,0:T(8,128)(2,1)} %get-tuple-element.16.dgu, ...), custom_call_target="tpu_custom_call" | custom-call | tf_op jit(solution)/shard_map/pallas_call | solution.py:677

commit v5 on v4

--- a/solution.py
+++ b/solution.py
@@ -24,16 +24,17 @@
 SPLIT_R = (32, 48, 48)
 
 GATHER = (
-    "yc", "zb0", "wl", "zc0", "xab", "rt", "yc", "zb0", "zc1", "zc2", "-8", "yc", "px0", "zc3", "zc0", "xab", "zb2",
-    "zb1", "wl", "rt", "xab", "zb3", "ya", "py0", "zb0", "-13", "zc1", "rt", "zc2", "zc3", "px1", "ya", "px2", "-8",
-    "px0", "zc0", "rt", "zb2", "ya", "-8", "zb1", "zb3", "za", "py2", "py1", "zb0", "-8", "py0", "zc1", "-5", "px1",
-    "zc2", "zc3", "px4", "px3", "zc0", "zb2", "py2", "zb1", "px2", "zb3", "py4", "py3", "-13", "px0", "py1", "rt",
-    "route", "py0", "pick0", "px1", "acc0", "-6", "py2", "za", "zb0", "-8", "zc1", "px4", "py4", "-6", "zc2", "zc3",
-    "px5", "px6", "zc0", "-8", "zb2", "py3", "zb1", "px3", "-8", "zb3", "py5", "py6", "py1", "pick1", "px2",
-    "pick2", "py4", "acc1", "acc2", "px4", "-4", "py3", "za", "px5", "zc1", "pick4", "zc2", "py5", "zc3", "px8",
-    "px7", "zb2", "acc4", "zb1", "zb3", "py8", "py7", "-16", "py6", "px6", "-14", "py5", "px3", "pick3", "acc3",
-    "py8", "px5", "-6", "py7", "za", "pick5", "px8", "py6", "acc5", "py8", "-8", "px7", "py7", "-8", "px6", "pick6",
-    "acc6", "px8", "za", "-6", "px7", "pick7", "acc7",
+    "zb0", "yc", "zc0", "pq0", "xab", "wl", "rt", "zb0", "yc", "pq1", "pq2", "zc2", "pq0", "zc0", "yc", "pq3",
+    "zc1", "zc3", "rt", "xab", "zb2", "zb1", "wl", "-8", "zb0", "xab", "zb3", "ya", "py0", "zc2", "pq1", "rt", "-8",
+    "zc0", "pq2", "-8", "pq0", "zc1", "-14", "pq3", "zc3", "px1", "pq1", "ya", "px2", "rt", "zb2", "-4", "pq2",
+    "zb1", "ya", "-5", "pq3", "zb0", "zb3", "za", "py2", "py1", "-8", "zc2", "-4", "py0", "zc0", "-7", "zc1", "px1",
+    "zc3", "px4", "px3", "zb2", "zb1", "py2", "zb0", "zb3", "px2", "py3", "py4", "-8", "rt", "route", "gcol", "py1",
+    "px1", "py0", "pick0", "acc0", "-8", "py2", "za", "px4", "-11", "zc2", "zc0", "py3", "zc1", "-8", "zc3", "px6",
+    "px5", "-4", "px3", "zb2", "-8", "zb1", "py4", "zb3", "py6", "py5", "px2", "pick2", "acc2", "py1", "pick1",
+    "acc1", "py3", "px4", "py4", "px6", "-8", "za", "pick4", "acc4", "zc2", "zc1", "py6", "zc3", "px7", "zb2",
+    "px8", "zb1", "-8", "zb3", "py7", "py8", "px5", "-16", "py5", "px3", "pick3", "acc3", "py6", "px6", "py7", "-8",
+    "px7", "za", "py8", "pick6", "acc6", "px8", "py5", "-12", "py7", "px5", "py8", "pick5", "acc5", "px7", "-8",
+    "px8", "za", "pick7", "acc7",
 )
 SCATTER = (
     "make7", "sza", "ry7", "rx7", "make6", "ry6", "rx6", "make5", "sza", "ry5", "rx5", "make4", "ry7", "ry4", "rx7",
@@ -199,7 +200,7 @@
     return out
 
 
-N_SEM = 320
+N_SEM = 340
 N_LOC = 32
 
 
@@ -209,7 +210,7 @@
     tok_in, grad_in, ids_in, gates_in, wg_in, wu_in, wd_in = take(7)
     tok_out, gg_out, dgu_out, dd_out = take(4)
     buf, xs, gxs, wgu, wd, sel, selt, part = take(8)
-    agu, araw, pgu, sh, gp, member, target, gatev = take(8)
+    agu, araw, pgu, sh, gp, gatecol, member, target, gatev = take(9)
     rt, ggd, gg_rx, gg_rz = take(4)
     osg, osd, org, ord_ = take(4)
     stg, std = take(2)
@@ -370,10 +371,19 @@
     for k, d in enumerate((0, 1, 3, 2)):
         ring_task(f"zb{k}", column_b(lax.rem(x + d, 4)))
         ring_task(f"zc{k}", column_c(lax.rem(y + d, 4)))
+    for k, d in enumerate((0, 1, 3, 2)):
+        py = lax.rem(y + d, 4)
+        ring_task(f"pq{k}", ring4_gather(
+            net, x,
+            lambda i, py=py: buf.at[i, py, z, gc],
+            lambda i, py=py: buf.at[i, py, z, sz(ra + rb, hc)],
+            lambda i, py=py: buf.at[i, py, z, sz(ra + rb + hc, rc - hc)],
+            xr, xl))
     for k, zz in enumerate(zs):
         for h in range(1 + k // 7):
             gx, gy = half_plane(zz, h) if k == 7 else plane(zz)
-            ring_task(f"px{k + h}", gx)
+            if k > 0:
+                ring_task(f"px{k + h}", gx)
             ring_task(f"py{k + h}", gy)
     ring_task("rt", route_ring())
     ring_task("wl", load_weights())
@@ -437,6 +447,14 @@
         for e in range(E4):
             body(e)
 
+    def gate_columns(e):
+        for p in range(PAIRS):
+            for k in range(2):
+                s = sel[p, pl.ds(pl.multiple_of(e * 48, 16), 48), k * TOK : (k + 1) * TOK].astype(F32)
+                g = gatev[pl.ds(e * 16 + 2 * p + k, 1), :]
+                col = jnp.sum((s * g)[k * CAP : (k + 1) * CAP], axis=1, keepdims=True)
+                gatecol[e, pl.ds(p * 48 + k * CAP, CAP), :] = jnp.broadcast_to(col, (CAP, H))
+
     def forward(e):
         gu, raw = agu[e], araw[e]
         gate_pre, up_pre = gu[:, :H], gu[:, H:]
@@ -444,13 +462,7 @@
         swish = gate_pre * sig
         hidden = swish * up_pre
         gp[e] = jnp.broadcast_to(jnp.sum(hidden * raw, axis=1, keepdims=True), (ROWS, H))
-        cols = []
-        for p in range(PAIRS):
-            for k in range(2):
-                s = sel[p, pl.ds(pl.multiple_of(e * 48, 16), 48), k * TOK : (k + 1) * TOK].astype(F32)
-                g = gatev[pl.ds(e * 16 + 2 * p + k, 1), :]
-                cols.append(jnp.sum((s * g)[k * CAP : (k + 1) * CAP], axis=1, keepdims=True))
-        gate = jnp.concatenate(cols, axis=0)
+        gate = gatecol[e]
         hg = gate * raw
         pgu[e, :, H:] = (hg * swish).astype(BF)
         pgu[e, :, :H] = (hg * up_pre * sig * (1.0 + gate_pre * (1.0 - sig))).astype(BF)
@@ -502,6 +514,7 @@
                 tasks[name]()
 
     tasks["route"] = route
+    tasks["gcol"] = lambda: loop(E4, gate_columns)
     for k, zz in enumerate(zs):
         tasks[f"pick{k}"] = functools.partial(pick, zz)
         tasks[f"acc{k}"] = functools.partial(accumulate, zz, k == 0)
@@ -669,7 +682,7 @@
 
 
 def finish(tok, gg, dgu, dd):
-    steps = 4
+    steps = 8
     n = D // steps
     whole = lambda i: (0, 0)
     rows = lambda i: (0, i, 0)
@@ -717,6 +730,7 @@
         pltpu.VMEM((E4, ROWS, H), F32),
         pltpu.VMEM((E4, ROWS, 2 * H), BF),
         pltpu.VMEM((E4, ROWS, H), BF),
+        pltpu.VMEM((E4, ROWS, H), F32),
         pltpu.VMEM((E4, ROWS, H), F32),
         pltpu.VMEM((64, TOK), F32),
         pltpu.VMEM((64, TOK), F32),

time: 139 us -> 139 us (level)
    pallas_call x1, Pallas kernels: 5.03 us -> 6.65 us  [finish(): pl.pallas_call(finish_kernel, grid=(steps,), in_specs=[pl.BlockSpec((TOK,...]
where the time goes in v5:
time: 139 us
  Pallas kernels  139 us (100%)
    pallas_call x1, Pallas kernels, local(): pl.pallas_call(kernel, out_shape=(jax.ShapeDtypeStruct((TOK, W), BF), jax...  132 us
    pallas_call x1, Pallas kernels, finish(): pl.pallas_call(finish_kernel, grid=(steps,), in_specs=[pl.BlockSpec((TOK,...  6.65 us

profile of v5, /device:TPU:32, one launch (start us, length us, event | category | flops | bytes accessed | tf_op | source)
XLA Modules:
  0.0 139.2 jit_solution(15439432203621333679)
XLA Ops:
  0.6 131.9 %shard_map.110 = (bf16[128,256]{1,0:T(8,128)(2,1)}, f32[8,128]{1,0:T(8,128)}, bf16[2,2048,256]{2,1,0:T(8,128)(2,1)}, bf16[2,128,2048]{2,1,0:T(8,128)(2,1)}) custom-call(bf16[128,256]{1,0:T(8,128)(2,1)} %refs_0_.1, bf16[128,256]{1,0:T(8,128)(2,1)} %refs_1_.1, s32[8,128]{1,0:T(8,128)} %bitcast.3, bf16[8,128]{1,0:T(8,128)(2,1)} %bitcast.4, ...), custom_call_target="tpu_custom_call" | custom-call | tf_op jit(solution)/shard_map/pallas_call | solution.py:759
  132.6 6.6 %shard_map.111 = (bf16[128,256]{1,0:T(8,128)(2,1)}, f32[8,128]{1,0:T(8,128)}, f32[2,2048,128]{2,1,0:T(8,128)}, f32[2,2048,128]{2,1,0:T(8,128)}, f32[2,128,2048]{2,1,0:T(8,128)}) custom-call(bf16[128,256]{1,0:T(8,128)(2,1)} %get-tuple-element.14.tok, f32[8,128]{1,0:T(8,128)} %get-tuple-element.15.gg, bf16[2,2048,256]{2,1,0:T(8,128)(2,1)} %get-tuple-element.16.dgu, ...), custom_call_target="tpu_custom_call" | custom-call | tf_op jit(solution)/shard_map/pallas_call | solution.py:690

commit v6 on v5

--- a/solution.py
+++ b/solution.py
@@ -673,36 +673,55 @@
     net.drain()
 
 
-def finish_kernel(tok, gg, dgu, dd, tok_out, gg_out, dg_out, du_out, dd_out):
-    tok_out[...] = tok[...]
-    gg_out[...] = gg[...]
-    dg_out[...] = dgu[:, :, :H].astype(F32)
-    du_out[...] = dgu[:, :, H:].astype(F32)
-    dd_out[...] = dd[...].astype(F32)
+CHUNKS = 4
+
+
+def finish_kernel(tok, gg, dgu, dd, tok_out, gg_out, dg_out, du_out, dd_out, in_gu, in_d, out_g, out_u, out_d, in_sem, out_sem):
+    n = D // CHUNKS
+    small = [
+        pltpu.make_async_copy(tok, tok_out, out_sem.at[CHUNKS, 0]),
+        pltpu.make_async_copy(gg, gg_out, out_sem.at[CHUNKS, 1]),
+    ]
+    loads, stores = [], []
+    for m in range(CHUNKS):
+        f = slice(m * n, (m + 1) * n)
+        loads.append((
+            pltpu.make_async_copy(dgu.at[:, f, :], in_gu.at[m], in_sem.at[m, 0]),
+            pltpu.make_async_copy(dd.at[:, :, f], in_d.at[m], in_sem.at[m, 1]),
+        ))
+        stores.append((
+            pltpu.make_async_copy(out_g.at[m], dg_out.at[:, f, :], out_sem.at[m, 0]),
+            pltpu.make_async_copy(out_u.at[m], du_out.at[:, f, :], out_sem.at[m, 1]),
+            pltpu.make_async_copy(out_d.at[m], dd_out.at[:, :, f], out_sem.at[m, 2]),
+        ))
+    for pair in loads:
+        for c in pair:
+            c.start()
+    for c in small:
+        c.start()
+    for m in range(CHUNKS):
+        loads[m][0].wait()
+        out_g[m] = in_gu[m, :, :, :H].astype(F32)
+        stores[m][0].start()
+        out_u[m] = in_gu[m, :, :, H:].astype(F32)
+        stores[m][1].start()
+        loads[m][1].wait()
+        out_d[m] = in_d[m].astype(F32)
+        stores[m][2].start()
+    for c in small:
+        c.wait()
+    for group in stores:
+        for c in group:
+            c.wait()
 
 
 def finish(tok, gg, dgu, dd):
-    steps = 8
-    n = D // steps
-    whole = lambda i: (0, 0)
-    rows = lambda i: (0, i, 0)
-    cols = lambda i: (0, 0, i)
+    n = D // CHUNKS
+    any_spec = pl.BlockSpec(memory_space=pl.ANY)
     return pl.pallas_call(
         finish_kernel,
-        grid=(steps,),
-        in_specs=[
-            pl.BlockSpec((TOK, W), whole),
-            pl.BlockSpec((8, TOK), whole),
-            pl.BlockSpec((2, n, 2 * H), rows),
-            pl.BlockSpec((2, H, n), cols),
-        ],
-        out_specs=[
-            pl.BlockSpec((TOK, W), whole),
-            pl.BlockSpec((8, TOK), whole),
-            pl.BlockSpec((2, n, H), rows),
-            pl.BlockSpec((2, n, H), rows),
-            pl.BlockSpec((2, H, n), cols),
-        ],
+        in_specs=[any_spec] * 4,
+        out_specs=[any_spec] * 5,
         out_shape=(
             jax.ShapeDtypeStruct((TOK, W), BF),
             jax.ShapeDtypeStruct((8, TOK), F32),
@@ -710,6 +729,15 @@
             jax.ShapeDtypeStruct((2, D, H), F32),
             jax.ShapeDtypeStruct((2, H, D), F32),
         ),
+        scratch_shapes=[
+            pltpu.VMEM((CHUNKS, 2, n, 2 * H), BF),
+            pltpu.VMEM((CHUNKS, 2, H, n), BF),
+            pltpu.VMEM((CHUNKS, 2, n, H), F32),
+            pltpu.VMEM((CHUNKS, 2, n, H), F32),
+            pltpu.VMEM((CHUNKS, 2, H, n), F32),
+            pltpu.SemaphoreType.DMA((CHUNKS, 2)),
+            pltpu.SemaphoreType.DMA((CHUNKS + 1, 3)),
+        ],
         compiler_params=pltpu.CompilerParams(vmem_limit_bytes=62 * 1024 * 1024),
     )(tok, gg, dgu, dd)
 

time: 139 us -> 137 us (0.986)
  Pallas kernels: 139 us -> 136 us
    pallas_call x1, Pallas kernels: 6.65 us -> 3.93 us  [finish(): pl.pallas_call(finish_kernel, in_specs=[any_spec] * 4, out_specs=[any_spe...]
where the time goes in v6:
time: 137 us
  Pallas kernels  136 us (99%)
    pallas_call x1, Pallas kernels, local(): pl.pallas_call(kernel, out_shape=(jax.ShapeDtypeStruct((TOK, W), BF), jax...  132 us
    pallas_call x1, Pallas kernels, finish(): pl.pallas_call(finish_kernel, in_specs=[any_spec] * 4, out_specs=[any_spe...  3.93 us

profile of v6, /device:TPU:32, one launch (start us, length us, event | category | flops | bytes accessed | tf_op | source)
XLA Modules:
  0.0 136.7 jit_solution(12102026062821857665)
XLA Ops:
  0.6 131.9 %shard_map.110 = (bf16[128,256]{1,0:T(8,128)(2,1)}, f32[8,128]{1,0:T(8,128)}, bf16[2,2048,256]{2,1,0:T(8,128)(2,1)}, bf16[2,128,2048]{2,1,0:T(8,128)(2,1)}) custom-call(bf16[128,256]{1,0:T(8,128)(2,1)} %refs_0_.1, bf16[128,256]{1,0:T(8,128)(2,1)} %refs_1_.1, s32[8,128]{1,0:T(8,128)} %bitcast.3, bf16[8,128]{1,0:T(8,128)(2,1)} %bitcast.4, ...), custom_call_target="tpu_custom_call" | custom-call | tf_op jit(solution)/shard_map/pallas_call | solution.py:787
  132.6 3.9 %shard_map.111 = (bf16[128,256]{1,0:T(8,128)(2,1)}, f32[8,128]{1,0:T(8,128)}, f32[2,2048,128]{2,1,0:T(8,128)}, f32[2,2048,128]{2,1,0:T(8,128)}, f32[2,128,2048]{2,1,0:T(8,128)}) custom-call(bf16[128,256]{1,0:T(8,128)(2,1)} %get-tuple-element.14.tok, f32[8,128]{1,0:T(8,128)} %get-tuple-element.15.gg, bf16[2,2048,256]{2,1,0:T(8,128)(2,1)} %get-tuple-element.16.dgu, ...), custom_call_target="tpu_custom_call" | custom-call | tf_op jit(solution)/shard_map/pallas_call | solution.py:721
